TPU v7x, 32 devices: a whole 2x2x4 slice. The times are simulated.
32 devices in a mesh: groups: 2 (over y), pool: 16 (over z, x, core).
Axes of the slice: x: 2, y: 2, z: 4, core: 2. Of those that a mesh axis runs over, the one named last changes fastest.
Arguments:
- anchors: bfloat16 [4096, 1024], P(('groups', 'pool')), parts along dimension 0, may hold values from -7 to 7
- deltas: bfloat16 [4096, 15, 1024], P(('groups', 'pool')), parts along dimension 0, may hold values from -5 to 5
- scales: float32 [4096, 8], P(('groups', 'pool')), parts along dimension 0, may hold values from 0.15 to 0.8
- queries: bfloat16 [32, 8, 8192], P('groups'), parts along dimension 0, may hold values from -7 to 7
- lengths: int32 [32], P('groups'), parts along dimension 0, may hold values from 64 to 192, as said below
- page_owner: int32 [4096], P('groups'), parts along dimension 0, may hold values from 0 to 15, as said below
Outputs:
- decoded_cache: bfloat16 [4096, 16, 1024], P(('groups', 'pool')), parts along dimension 0
- attention: bfloat16 [32, 8, 8192], P('groups', None, 'pool'), parts along dimension 0
There are 2 independent parts, one for each index of `groups`. A program takes and returns all parts, laid end to end along the dimension named above; each array names one. Nothing has to cross between parts.
Inputs may be any that keep to these rules, and one draw needn't show every extreme that they name: `lengths`: pages of each request; together they cover all 2048 pages of the group. `page_owner`: each prefill device sends either none or exactly 16 of its pages to each decode device, and each decode device owns exactly 128 pages.
All inputs are finite; a program needn't handle non-finite values.
Results may differ from a plain program's by a relative error of at most 0.0046.
Values may be sent and summed in bfloat16 or wider, within the bound.
No kernel may reach another device: no remote copies, remote signals or barrier semaphores. Data moves between devices by JAX's collectives and lax.ppermute only.
A program may use at most 192 MiB of HBM per device.

v0:
```python
import functools
import jax
import jax.numpy as jnp
from jax import lax
from jax.experimental import pallas as pl
from jax.experimental.pallas import tpu as pltpu
from jax.sharding import PartitionSpec as P

QH = 64
KVH = 4
HD = 128
PAGE = 16
STEPS = 8
REQS = 16
KVW = 2 * KVH * HD
SPAN = 3
LOW = -1e30
VMEM_LIMIT = 48 * 1024 * 1024
F32 = jnp.float32
BF16 = jnp.bfloat16
I32 = jnp.int32


def decode_kernel(chunk, place, flags, blocks, anchors, deltas, scales, out, rows, staged, sems):
    step = pl.program_id(0)
    for head in range(2 * KVH):
        cols = slice(head * HD, (head + 1) * HD)
        scale = jnp.broadcast_to(scales[:, head : head + 1], (chunk, HD))
        anchor = anchors[:, cols].astype(F32)
        rows[head * PAGE * chunk : head * PAGE * chunk + chunk, :] = anchor
        for token in range(1, PAGE):
            start = (head * PAGE + token) * chunk
            rows[start : start + chunk, :] = anchor + scale * deltas[token - 1, :, cols].astype(F32)
    for page in range(chunk):
        picked = [
            rows[pl.ds(head * PAGE * chunk + page, PAGE, stride=chunk), :]
            for head in range(2 * KVH)
        ]
        staged[place[step * chunk + page]] = jnp.concatenate(picked, axis=1).astype(BF16)

    @pl.when(step == pl.num_programs(0) - 1)
    def flush():
        copies = []
        for owner in range(16):
            copy = pltpu.make_async_copy(
                staged.at[pl.ds(blocks[owner] * PAGE, PAGE)],
                out.at[pl.ds(owner * PAGE, PAGE)],
                sems.at[owner],
            )
            pl.when(flags[owner] > 0)(copy.start)
            copies.append(copy)
        for owner in range(16):
            pl.when(flags[owner] > 0)(copies[owner].wait)


def decode_sorted(place, flags, blocks, anchors, deltas, scales):
    number = anchors.shape[0]
    chunk = 16
    return pl.pallas_call(
        functools.partial(decode_kernel, chunk),
        grid_spec=pltpu.PrefetchScalarGridSpec(
            num_scalar_prefetch=3,
            grid=(number // chunk,),
            in_specs=[
                pl.BlockSpec((chunk, KVW), lambda i, *_: (i, 0)),
                pl.BlockSpec((PAGE - 1, chunk, KVW), lambda i, *_: (0, i, 0)),
                pl.BlockSpec((chunk, 2 * KVH), lambda i, *_: (i, 0)),
            ],
            out_specs=pl.BlockSpec(memory_space=pl.ANY),
            scratch_shapes=[
                pltpu.VMEM((2 * KVH * PAGE * chunk, HD), F32),
                pltpu.VMEM((number, PAGE, KVW), BF16),
                pltpu.SemaphoreType.DMA((16,)),
            ],
        ),
        out_shape=jax.ShapeDtypeStruct((16 * PAGE, PAGE, KVW), BF16),
        compiler_params=pltpu.CompilerParams(vmem_limit_bytes=VMEM_LIMIT),
        name="decode_sorted",
    )(place, flags, blocks, anchors, deltas, scales)


def attend_kernel(head, plan, requests, first, second, third, key_anchor, val_anchor, key_delta, val_delta, scales, after, out, keys, vals):
    number = key_anchor.shape[0]
    columns = jnp.transpose(scales[...])
    key_scale = columns[:, head : head + 1]
    val_scale = columns[:, head + KVH : head + KVH + 1]
    for anchor, delta, scale, kept in (
        (key_anchor, key_delta, key_scale, keys),
        (val_anchor, val_delta, val_scale, vals),
    ):
        kept[0:number, :] = anchor[...]
        wide = anchor[...].astype(F32)
        for token in range(1, PAGE):
            kept[token * number : (token + 1) * number, :] = (
                wide + scale * delta[token - 1].astype(F32)
            ).astype(BF16)
    token_request = jnp.concatenate([requests[4:5, :]] * PAGE, axis=1) - plan[5, 0]
    rows = STEPS * QH // KVH
    eye = lax.broadcasted_iota(I32, (rows, rows), 0) == lax.broadcasted_iota(I32, (rows, rows), 1)
    pieces = []
    for slot, queries in enumerate((first, second, third)):
        wide = queries[0].astype(F32)
        picked = jnp.concatenate(
            [wide[:, group * HD : (group + 1) * HD] for group in range(QH // KVH)], axis=0
        ).astype(BF16)
        scores = lax.dot_general(
            picked, keys[...], (((1,), (1,)), ((), ())), preferred_element_type=F32
        ) * HD ** (-0.5)
        inside = token_request == slot
        scores = jnp.where(inside, scores, LOW)
        top = jnp.max(scores, axis=1, keepdims=True)
        exponent = jnp.where(inside, jnp.exp(scores - top), 0.0)
        total = jnp.maximum(jnp.sum(exponent, axis=1, keepdims=True), 1e-30)
        numer = jnp.dot(exponent.astype(BF16), vals[...], preferred_element_type=F32)
        mean = (numer * (1.0 / total)).astype(BF16)
        quarter = rows // 4
        for part in range(4):
            out[part, slot * quarter : (slot + 1) * quarter, :] = mean[
                part * quarter : (part + 1) * quarter
            ]
        level = top + jnp.log(total)
        line = jnp.sum(jnp.where(eye, level, 0.0), axis=0, keepdims=True)
        for _ in range(3):
            piece = line.astype(BF16).astype(F32)
            pieces.append(piece)
            line = line - piece
    pieces.append(jnp.zeros((16 - len(pieces), rows), F32))
    stats = jnp.concatenate(pieces, axis=0).astype(BF16)
    for part in range(4):
        out[part, 96:112, :] = stats


def attend(head, plan, queries, anchors, deltas, scales, after):
    number = anchors.shape[0]
    rows = STEPS * QH // KVH
    return pl.pallas_call(
        functools.partial(attend_kernel, head),
        grid_spec=pltpu.PrefetchScalarGridSpec(
            num_scalar_prefetch=1,
            grid=(1,),
            in_specs=[
                pl.BlockSpec((8, number), lambda i, *_: (0, 0)),
                *[
                    pl.BlockSpec((1, STEPS, rows * HD // STEPS), lambda i, p, k=k: (p[5, 0] + k, 0, head))
                    for k in range(SPAN)
                ],
                pl.BlockSpec((number, HD), lambda i, *_: (0, head)),
                pl.BlockSpec((number, HD), lambda i, *_: (0, head + KVH)),
                pl.BlockSpec((PAGE - 1, number, HD), lambda i, *_: (0, 0, head)),
                pl.BlockSpec((PAGE - 1, number, HD), lambda i, *_: (0, 0, head + KVH)),
                pl.BlockSpec((2 * KVH, number), lambda i, *_: (0, 0)),
                pl.BlockSpec(memory_space=pl.ANY),
            ],
            out_specs=pl.BlockSpec((4, 112, HD), lambda i, *_: (head, 0, 0)),
            scratch_shapes=[
                pltpu.VMEM((PAGE * number, HD), BF16),
                pltpu.VMEM((PAGE * number, HD), BF16),
            ],
        ),
        out_shape=jax.ShapeDtypeStruct((16, 112, HD), BF16),
        input_output_aliases={} if head == 0 else {10: 0},
        compiler_params=pltpu.CompilerParams(vmem_limit_bytes=VMEM_LIMIT),
        name=f"attend_{head}",
    )(plan, plan, queries, queries, queries, anchors, anchors, deltas, deltas, scales, after)


def merge_kernel(plan, place, parts, after, out, level, top, total, numer):
    quarter = 32
    row = lax.broadcasted_iota(I32, (quarter, HD), 0)
    lane = lax.broadcasted_iota(I32, (quarter, HD), 1)
    mine = lane == row + quarter * ((place[0] & 1) * 2 + place[1])
    top[...] = jnp.full(top.shape, LOW, F32)
    total[...] = jnp.zeros(total.shape, F32)
    numer[...] = jnp.zeros(numer.shape, F32)
    for sender in range(16):
        stats = parts[sender, 96:112, :].astype(F32)
        for slot in range(SPAN):
            line = stats[3 * slot : 3 * slot + 1] + (
                stats[3 * slot + 1 : 3 * slot + 2] + stats[3 * slot + 2 : 3 * slot + 3]
            )
            column = jnp.sum(jnp.where(mine, line, 0.0), axis=1, keepdims=True)
            column = jnp.broadcast_to(column, (quarter, HD))
            level[sender * SPAN + slot] = column
            request = plan[3, sender] + slot
            top[request] = jnp.maximum(top[request], column)
    for sender in range(16):
        for slot in range(SPAN):
            request = plan[3, sender] + slot
            weight = jnp.exp(level[sender * SPAN + slot] - top[request])
            mean = parts[sender, slot * quarter : (slot + 1) * quarter, :].astype(F32)
            total[request] += weight
            numer[request] += weight * mean
    for request in range(REQS):
        result = (numer[request] / total[request]).astype(BF16)
        for group in range(4):
            out[request, :, group * HD : (group + 1) * HD] = result[
                group * STEPS : (group + 1) * STEPS
            ]


def merge(plan, place, parts, after):
    return pl.pallas_call(
        merge_kernel,
        grid_spec=pltpu.PrefetchScalarGridSpec(
            num_scalar_prefetch=2,
            grid=(1,),
            in_specs=[
                pl.BlockSpec((16, 112, HD), lambda i, *_: (0, 0, 0)),
                pl.BlockSpec(memory_space=pl.ANY),
            ],
            out_specs=pl.BlockSpec((REQS, STEPS, 4 * HD), lambda i, *_: (0, 0, 0)),
            scratch_shapes=[
                pltpu.VMEM((16 * SPAN, 32, HD), F32),
                pltpu.VMEM((REQS, 32, HD), F32),
                pltpu.VMEM((REQS, 32, HD), F32),
                pltpu.VMEM((REQS, 32, HD), F32),
            ],
        ),
        out_shape=jax.ShapeDtypeStruct((REQS, STEPS, 4 * HD), BF16),
        compiler_params=pltpu.CompilerParams(vmem_limit_bytes=VMEM_LIMIT),
        name="merge",
    )(plan, place, parts, after)


def assemble_kernel(flags, blocks, arrived, out, staged, in_sems, out_sems):
    reads, writes = [], []
    for sender in range(16):
        rows = pl.ds(blocks[sender] * PAGE, PAGE)
        source = arrived.at[pl.ds(sender * PAGE, PAGE)]
        reads.append(pltpu.make_async_copy(source, staged.at[rows], in_sems.at[sender]))
        writes.append(pltpu.make_async_copy(staged.at[rows], out.at[rows], out_sems.at[sender]))
    for sender in range(16):
        pl.when(flags[sender] > 0)(reads[sender].start)
    for sender in range(16):

        @pl.when(flags[sender] > 0)
        def forward():
            reads[sender].wait()
            writes[sender].start()

    for sender in range(16):
        pl.when(flags[sender] > 0)(writes[sender].wait)


def assemble(flags, blocks, arrived, number):
    return pl.pallas_call(
        assemble_kernel,
        grid_spec=pltpu.PrefetchScalarGridSpec(
            num_scalar_prefetch=2,
            grid=(1,),
            in_specs=[pl.BlockSpec(memory_space=pl.ANY)],
            out_specs=pl.BlockSpec(memory_space=pl.ANY),
            scratch_shapes=[
                pltpu.VMEM((number, PAGE, KVW), BF16),
                pltpu.SemaphoreType.DMA((16,)),
                pltpu.SemaphoreType.DMA((16,)),
            ],
        ),
        out_shape=jax.ShapeDtypeStruct((number, PAGE, KVW), BF16),
        compiler_params=pltpu.CompilerParams(vmem_limit_bytes=VMEM_LIMIT),
        name="assemble",
    )(flags, blocks, arrived)


ROUNDS = 9
LIMIT = 10
UNIT = 2
LAG = 2
SIDE_LAG = 3
SLOTS = 7
SIDE = (3, 0, 3, 0, 3, 0, 2, 2, 1)
HALF = PAGE // 2
FAR = 1e6


def units_of(port, time):
    if port < 2:
        return UNIT
    return SIDE[time] if time < len(SIDE) else 2


def plan_kernel(place, lengths, owners, out):
    chip = place[0]
    row = lax.broadcasted_iota(I32, (16, 128), 0)
    lanes = lax.broadcasted_iota(I32, (16, 128), 1)
    sender_of = lanes >> 3
    turn = (lanes & 7).astype(F32)
    table = owners[...]
    running = jnp.zeros((16, 1), F32)
    sends = []
    targets = jnp.zeros((16, 128), F32)
    for owner in range(16):
        flag = jnp.max(jnp.where(table == owner, 1.0, 0.0), axis=1, keepdims=True)
        targets += jnp.where(turn == running, flag * owner, 0.0)
        sends.append(flag)
        running = running + flag
    dest = jnp.sum(jnp.where(row == sender_of, targets, 0.0), axis=0, keepdims=True)
    hits = jnp.zeros((16, 128), F32)
    for owner in range(16):
        hits += sends[owner] * jnp.where(dest == owner, 1.0, 0.0)
    rank = jnp.sum(jnp.where(row < sender_of, hits, 0.0), axis=0, keepdims=True).astype(I32)
    dest = dest.astype(I32)
    lane = lax.broadcasted_iota(I32, (1, 128), 1)
    sender = lane >> 3
    from_z, from_x = sender >> 2, (sender >> 1) & 1
    to_z, to_x = dest >> 2, (dest >> 1) & 1
    crosses = (from_z >> 1) != (to_z >> 1)
    below = jnp.where(
        lax.broadcasted_iota(I32, (128, 128), 0) < lax.broadcasted_iota(I32, (128, 128), 1), 1.0, 0.0
    )
    line = from_x
    for side in range(2):
        leaving = crosses & ((from_z >> 1) == side)
        free = jnp.where(leaving & (from_x != to_x), 1.0, 0.0)
        fixed = jnp.where(leaving & (from_x == to_x), 1.0, 0.0)
        tilt = jnp.sum(fixed * (2 * from_x - 1).astype(F32), axis=1, keepdims=True)
        count = jnp.sum(free, axis=1, keepdims=True)
        share = jnp.clip(jnp.floor((tilt + count) * 0.5), 0.0, count)
        step = share / jnp.maximum(count, 1.0)
        index = jnp.dot(jnp.broadcast_to(free, (8, 128)), below, preferred_element_type=F32)[0:1]
        first = jnp.floor((index + 1.0) * step + 1e-3) > jnp.floor(index * step + 1e-3)
        line = jnp.where(free > 0.0, jnp.where(first, 0, 1), line)
    chips = lax.broadcasted_iota(I32, (8, 128), 0)
    mine = lax.broadcasted_iota(I32, (8, 1), 0) == chip

    def round_step(time, carry):
        at_z, at_x, ready, code, steps, needed = carry
        waits = crosses & ((at_z >> 1) == (from_z >> 1))
        turns = ((at_z == to_z) & (at_x != to_x)) | (waits & (line != at_x))
        along = jnp.logical_not(turns) & (at_z != to_z)
        left = jnp.abs(to_z - at_z) + jnp.where(at_x != to_x, 1, 0)
        key = ((8 - left) * 128 + lane).astype(F32)
        here = (at_z * 2 + at_x == chips) & (ready <= time)
        heading = jnp.where(turns, 2, jnp.where(along, jnp.where(to_z > at_z, 0, 1), 3))
        moved = jnp.zeros((1, 128), F32)
        landed = jnp.zeros((1, 128), F32)
        value = (code + 1).astype(F32)
        side = sum(jnp.where(time == t, units_of(2, t), 0) for t in range(LIMIT))
        for port in range(3):
            keys = jnp.where(here & (heading == port), key, FAR)
            for unit in range(UNIT if port < 2 else 3):
                if port == 2:
                    keys = jnp.where(unit < side, keys, FAR)
                least = jnp.min(keys, axis=1, keepdims=True)
                chosen = jnp.where((keys == least) & (keys < FAR), 1.0, 0.0)
                source = jnp.sum(chosen * value, axis=1, keepdims=True)
                source = jnp.sum(jnp.where(mine, source, 0.0), axis=0, keepdims=True)
                slot = SLOTS * time + UNIT * port + unit
                steps = steps + jnp.where(lane == slot, source, 0.0)
                taken = jnp.sum(chosen, axis=0, keepdims=True)
                moved = moved + taken * (port + 1)
                landed = landed + taken * (slot + 16).astype(F32)
                keys = jnp.where(chosen > 0.0, FAR, keys)
        went = moved.astype(I32)
        at_z = at_z + jnp.where(went == 1, 1, 0) - jnp.where(went == 2, 1, 0)
        at_x = jnp.where(went == 3, 1 - at_x, at_x)
        ready = jnp.where(went > 0, time + jnp.where(went == 3, SIDE_LAG, LAG), ready)
        code = jnp.where(went > 0, landed.astype(I32), code)
        any_move = jnp.max(moved, axis=1, keepdims=True)
        needed = jnp.where(any_move > 0.0, (time + 1).astype(F32), needed)
        return at_z, at_x, ready, code, steps, needed

    start = (
        from_z,
        from_x,
        jnp.zeros((1, 128), I32),
        (sender & 1) * 8 + (lane & 7),
        jnp.zeros((1, 128), F32),
        jnp.zeros((1, 1), F32),
    )
    at_z, at_x, ready, code, steps, needed = lax.fori_loop(0, LIMIT, round_step, start)
    undone = jnp.where((at_z == to_z) & (at_x == to_x), 0.0, 1.0)
    undone = jnp.max(undone, axis=1, keepdims=True)
    needed = jnp.where(undone > 0.0, float(LIMIT + 1), needed)
    arrives = (dest >> 1) == chip
    slots = (dest & 1) * 8 + rank
    final = jnp.sum(
        jnp.where((row == slots) & arrives, (code + 1).astype(F32), 0.0), axis=1, keepdims=True
    )
    final = jnp.sum(jnp.where(row == lanes, final, 0.0), axis=0, keepdims=True)
    out[0:1, :] = steps.astype(I32)
    out[1:2, :] = final.astype(I32)
    out[2:3, :] = jnp.broadcast_to(needed, (1, 128)).astype(I32)
    page = (2 * chip + place[1]) * 128 + lane
    requests = jnp.zeros((1, 128), I32)
    bases = jnp.zeros((1, 128), I32)
    end = 0
    for request in range(REQS):
        end = end + lengths[request]
        requests = requests + jnp.where(page >= end, 1, 0)
        bases = bases + jnp.where(lane * 128 >= end, 1, 0)
    bases = jnp.minimum(bases, REQS - SPAN)
    base = jnp.sum(jnp.where(lane == 2 * chip + place[1], bases, 0).astype(F32), axis=1, keepdims=True)
    out[3:4, :] = bases
    out[4:5, :] = requests
    out[5:6, :] = jnp.broadcast_to(base, (1, 128)).astype(I32)
    out[6:8, :] = jnp.zeros((2, 128), I32)


def make_plan(place, lengths, page_owner):
    return pl.pallas_call(
        plan_kernel,
        grid_spec=pltpu.PrefetchScalarGridSpec(
            num_scalar_prefetch=2,
            grid=(1,),
            in_specs=[pl.BlockSpec((16, 128), lambda i, *_: (0, 0))],
            out_specs=pl.BlockSpec((8, 128), lambda i, *_: (0, 0)),
        ),
        out_shape=jax.ShapeDtypeStruct((8, 128), I32),
        name="make_plan",
    )(place, lengths, page_owner.reshape(16, 128))


def halves_kernel(place, owners, anchors, deltas, scales, keep, give, swap, columns, ranks, order, rows, staged, sems):
    step = pl.program_id(0)
    count = PAGE * PAGE

    @pl.when(step == 0)
    def build():
        row = lax.broadcasted_iota(I32, (count, count), 0)
        lane = lax.broadcasted_iota(I32, (count, count), 1)
        swap[...] = jnp.where(lane == (row & 15) * PAGE + (row >> 4), 1.0, 0.0).astype(BF16)
        columns[...] = jnp.transpose(scales[...])
        number = owners.shape[1]
        row = lax.broadcasted_iota(I32, (number, number), 0)
        lane = lax.broadcasted_iota(I32, (number, number), 1)
        across = owners[pl.ds(2 * place[0] + place[1], 1), :].astype(F32)
        down = jnp.sum(jnp.where(row == lane, across, 0.0), axis=1, keepdims=True)
        ahead = (down < across) | ((down == across) & (row < lane))
        ranks[...] = jnp.sum(jnp.where(ahead, 1.0, 0.0), axis=0, keepdims=True).astype(I32)
        pltpu.make_async_copy(ranks, order, sems.at[2]).start()

    core = place[1]
    for part in range(anchors.shape[0] // PAGE):
        pages = slice(part * PAGE, (part + 1) * PAGE)
        for head in range(2 * KVH):
            cols = slice(head * HD, (head + 1) * HD)
            start = pl.multiple_of(step * anchors.shape[0] + part * PAGE, PAGE)
            scale = jnp.broadcast_to(columns[pl.ds(start, PAGE), head : head + 1], (PAGE, HD))
            first = anchors[pages, cols]
            anchor = first.astype(F32)
            rows[0:PAGE, cols] = first
            for token in range(1, PAGE):
                rebuilt = anchor + scale * deltas[token - 1, pages, cols].astype(F32)
                rows[token * PAGE : (token + 1) * PAGE, cols] = rebuilt.astype(BF16)
        turned = jnp.dot(swap[...], rows[...], preferred_element_type=F32).astype(BF16)
        if part == 0:

            @pl.when(step == 0)
            def ordered():
                pltpu.make_async_copy(ranks, order, sems.at[2]).wait()

        for page in range(PAGE):
            rank = order[0, step * anchors.shape[0] + part * PAGE + page]
            half = (rank >> 3) & 1
            slot = (half ^ core) * 64 + (rank >> 4) * HALF + (rank & 7)
            staged[slot] = turned[page * PAGE : (page + 1) * PAGE]

    @pl.when(step == pl.num_programs(0) - 1)
    def flush():
        copies = [
            pltpu.make_async_copy(staged.at[pl.ds(64, 64)], give, sems.at[0]),
            pltpu.make_async_copy(staged.at[pl.ds(0, 64)], keep, sems.at[1]),
        ]
        for copy in copies:
            copy.start()
        for copy in copies:
            copy.wait()


def decode_halves(place, page_owner, anchors, deltas, scales):
    number = anchors.shape[0]
    chunk = 2 * PAGE
    half = jax.ShapeDtypeStruct((number // 2, PAGE, KVW), BF16)
    return pl.pallas_call(
        halves_kernel,
        grid_spec=pltpu.PrefetchScalarGridSpec(
            num_scalar_prefetch=1,
            grid=(number // chunk,),
            in_specs=[
                pl.BlockSpec((16, number), lambda i, *_: (0, 0)),
                pl.BlockSpec((chunk, KVW), lambda i, *_: (i, 0)),
                pl.BlockSpec((PAGE - 1, chunk, KVW), lambda i, *_: (0, i, 0)),
                pl.BlockSpec((2 * KVH, number), lambda i, *_: (0, 0)),
            ],
            out_specs=[pl.BlockSpec(memory_space=pl.ANY)] * 2,
            scratch_shapes=[
                pltpu.VMEM((PAGE * PAGE, PAGE * PAGE), BF16),
                pltpu.VMEM((number, 2 * KVH), F32),
                pltpu.VMEM((1, number), I32),
                pltpu.SMEM((1, number), I32),
                pltpu.VMEM((PAGE * PAGE, KVW), BF16),
                pltpu.VMEM((number, PAGE, KVW), BF16),
                pltpu.SemaphoreType.DMA((3,)),
            ],
        ),
        out_shape=(half, half),
        compiler_params=pltpu.CompilerParams(vmem_limit_bytes=VMEM_LIMIT),
        name="decode_halves",
    )(place, page_owner.reshape(16, number), anchors, deltas, scales)


def fetch(code, core, own, landed, ports, target, sem):
    value = code - 1
    keep, got = own

    @pl.when((value >= 0) & (value < 16))
    def from_own():
        rows = pl.ds((value & 7) * HALF, HALF)

        @pl.when((value >> 3) == core)
        def kept():
            pltpu.make_async_copy(keep.at[rows], target, sem).start()

        @pl.when((value >> 3) != core)
        def gotten():
            pltpu.make_async_copy(got.at[rows], target, sem).start()

    for time, port, arrivals in landed:
        if port in ports:
            offset = value - 16 - SLOTS * time - UNIT * port

            @pl.when((offset >= 0) & (offset < units_of(port, time)))
            def from_round():
                rows = pl.ds(offset * HALF, HALF)
                pltpu.make_async_copy(arrivals.at[rows], target, sem).start()


def settle(code, own, target, sem):
    @pl.when(code > 0)
    def wait():
        pltpu.make_async_copy(own[0].at[pl.ds(0, HALF)], target, sem).wait()


def pick_kernel(time, tags, plan, place, *refs):
    own, landed = refs[:2], [tag + (ref,) for tag, ref in zip(tags, refs[2:])]
    used = [port for port in range(3) if units_of(port, time)]
    outs, sems = refs[-1 - len(used) : -1], refs[-1]
    for phase in range(2):
        for port, out in zip(used, outs):
            ports = (0, 1) if port == 2 else (port, 2)
            for unit in range(units_of(port, time)):
                code = plan[0, SLOTS * time + UNIT * port + unit]
                target = out.at[pl.ds(unit * HALF, HALF)]
                sem = sems.at[UNIT * port + unit]
                if phase == 0:
                    fetch(code, place[1], own, landed, ports, target, sem)
                else:
                    settle(code, own, target, sem)


def pick(time, plan, place, own, landed, after):
    landed = [item for item in landed if item[0] + (SIDE_LAG if item[1] == 2 else LAG) <= time]
    sources = list(own) + [item[2] for item in landed] + [after]
    pieces = [
        jax.ShapeDtypeStruct((units_of(port, time) * HALF, PAGE, KVW), BF16)
        for port in range(3)
        if units_of(port, time)
    ]
    return pl.pallas_call(
        functools.partial(pick_kernel, time, [item[:2] for item in landed]),
        grid_spec=pltpu.PrefetchScalarGridSpec(
            num_scalar_prefetch=2,
            grid=(1,),
            in_specs=[pl.BlockSpec(memory_space=pl.ANY)] * len(sources),
            out_specs=[pl.BlockSpec(piece.shape, lambda i, *_: (0, 0, 0)) for piece in pieces],
            scratch_shapes=[pltpu.SemaphoreType.DMA((SLOTS,))],
        ),
        out_shape=pieces,
        compiler_params=pltpu.CompilerParams(vmem_limit_bytes=VMEM_LIMIT),
        name=f"pick_{time}",
    )(plan, place, *sources)


def gather_kernel(mode, low, tags, plan, place, *refs):
    own, landed = refs[:2], [tag + (ref,) for tag, ref in zip(tags, refs[2:])]
    out, staged, in_sems, out_sems = refs[-4:]
    core = place[1]
    half = core if mode == "own" else 1 - core
    high = 16 + SLOTS * (1 + max(time for time, _ in tags))

    def code_of(slot):
        code = plan[1, half * 8 + slot]
        return jnp.where((code > low) & (code <= high), code, 0)

    def target_of(slot):
        return staged.at[pl.ds(slot * HALF, HALF)]

    def write_of(slot):
        start = slot * PAGE + core * HALF if mode == "own" else slot * HALF
        return pltpu.make_async_copy(
            target_of(slot), out.at[pl.ds(start, HALF)], out_sems.at[slot]
        )

    @pl.loop(0, 8)
    def read(slot):
        fetch(code_of(slot), core, own, landed, (0, 1, 2), target_of(slot), in_sems.at[slot])

    @pl.loop(0, 8)
    def forward(slot):
        settle(code_of(slot), own, target_of(slot), in_sems.at[slot])
        pl.when(code_of(slot) > 0)(write_of(slot).start)

    @pl.loop(0, 8)
    def close(slot):
        pl.when(code_of(slot) > 0)(write_of(slot).wait)


def gather(mode, low, plan, place, own, landed, after, base=None):
    sources = list(own) + [item[2] for item in landed] + [after]
    if base is not None:
        sources.append(base)
    pages = 8 * (PAGE if mode == "own" else HALF)
    return pl.pallas_call(
        functools.partial(gather_kernel, mode, low, [item[:2] for item in landed]),
        grid_spec=pltpu.PrefetchScalarGridSpec(
            num_scalar_prefetch=2,
            grid=(1,),
            in_specs=[pl.BlockSpec(memory_space=pl.ANY)] * len(sources),
            out_specs=pl.BlockSpec(memory_space=pl.ANY),
            scratch_shapes=[
                pltpu.VMEM((8 * HALF, PAGE, KVW), BF16),
                pltpu.SemaphoreType.DMA((8,)),
                pltpu.SemaphoreType.DMA((8,)),
            ],
        ),
        out_shape=jax.ShapeDtypeStruct((pages, PAGE, KVW), BF16),
        input_output_aliases={} if base is None else {1 + len(sources): 0},
        compiler_params=pltpu.CompilerParams(vmem_limit_bytes=VMEM_LIMIT),
        name=f"gather_{mode}",
    )(plan, place, *sources)


def fill_kernel(place, cache, other, out, staged, in_sems, out_sems):
    half = 1 - place[1]
    reads, writes = [], []
    for slot in range(8):
        rows = pl.ds(slot * HALF, HALF)
        reads.append(pltpu.make_async_copy(other.at[rows], staged.at[rows], in_sems.at[slot]))
        writes.append(
            pltpu.make_async_copy(
                staged.at[rows], out.at[pl.ds(slot * PAGE + half * HALF, HALF)], out_sems.at[slot]
            )
        )
    for read in reads:
        read.start()
    for read, write in zip(reads, writes):
        read.wait()
        write.start()
    for write in writes:
        write.wait()


def fill(place, cache, other):
    return pl.pallas_call(
        fill_kernel,
        grid_spec=pltpu.PrefetchScalarGridSpec(
            num_scalar_prefetch=1,
            grid=(1,),
            in_specs=[pl.BlockSpec(memory_space=pl.ANY)] * 2,
            out_specs=pl.BlockSpec(memory_space=pl.ANY),
            scratch_shapes=[
                pltpu.VMEM((8 * HALF, PAGE, KVW), BF16),
                pltpu.SemaphoreType.DMA((8,)),
                pltpu.SemaphoreType.DMA((8,)),
            ],
        ),
        out_shape=jax.ShapeDtypeStruct(cache.shape, cache.dtype),
        input_output_aliases={1: 0},
        compiler_params=pltpu.CompilerParams(vmem_limit_bytes=VMEM_LIMIT),
        name="fill",
    )(place, cache, other)


UP = tuple((i, i + 4) for i in range(12))
DOWN = tuple((i + 4, i) for i in range(12))
ACROSS = tuple((i, i ^ 2) for i in range(16))
TWIN = tuple((i, i ^ 1) for i in range(16))


def ship(time, parts):
    used = [port for port in range(3) if units_of(port, time)]
    hops = (UP, DOWN, ACROSS)
    return [(time, port, lax.ppermute(part, "pool", hops[port])) for port, part in zip(used, parts)]


def finish(plan, place, own, landed, after):
    give = gather("give", 0, plan, place, own, landed, after)
    other = lax.ppermute(give, "pool", TWIN)
    return fill(place, gather("own", 0, plan, place, own, landed, give), other)


def finish_in_two(plan, place, own, landed, after, attention):
    early = [item for item in landed if item[0] < ROUNDS - 1]
    last = [item for item in landed if item[0] >= ROUNDS - 1]
    low = 16 + SLOTS * (ROUNDS - 1)
    give = gather("give", 0, plan, place, own, early, after)
    keep = gather("own", 0, plan, place, own, early, after)
    keep, _ = lax.optimization_barrier((keep, attention))
    give = gather("give", low, plan, place, own, last, keep, give)
    other = lax.ppermute(give, "pool", TWIN)
    return fill(place, gather("own", low, plan, place, own, last, give, keep), other)


def local_lanes(anchors, deltas, scales, queries, lengths, page_owner):
    position = lax.axis_index("pool")
    number = anchors.shape[0]
    by_token = jnp.transpose(deltas, (1, 0, 2))
    place = jnp.stack([position >> 1, position & 1]).astype(I32)
    lines = jnp.transpose(scales)
    keep, give = decode_halves(place, page_owner, anchors, by_token, lines)
    got = lax.ppermute(give, "pool", TWIN)
    plan = make_plan(place, lengths, page_owner)
    own = (keep, got)
    landed = []
    after = partial = plan
    for time in range(ROUNDS):
        parts = pick(time, plan, place, own, landed, after)
        landed += ship(time, parts)
        after = parts[0]
        if 1 <= time <= KVH:
            seen, _ = lax.optimization_barrier((plan, after))
            after = partial = attend(time - 1, seen, queries, anchors, by_token, lines, partial)
    partial, _ = lax.optimization_barrier((partial, after))
    swapped = lax.all_to_all(partial, "pool", split_axis=0, concat_axis=0, tiled=True)
    attention = merge(plan, place, swapped, after)
    cache = finish_in_two(plan, place, own, landed, after, attention)

    def in_time(cache):
        return cache

    def late(cache):
        more, last = list(landed), plan
        for time in range(ROUNDS, LIMIT):
            parts = pick(time, plan, place, own, more, last)
            more += ship(time, parts)
            last = parts[0]
        return finish(plan, place, own, more, last)

    def padded(cache):
        owners = lax.dynamic_slice_in_dim(page_owner, position * number, number, 0)
        index = jnp.arange(number, dtype=I32)
        ahead = (owners[None, :] < owners[:, None]) | (
            (owners[None, :] == owners[:, None]) & (index[None, :] < index[:, None])
        )
        order = jnp.sum(ahead.astype(I32), axis=1)
        devices = jnp.arange(16, dtype=I32)
        sent = jnp.any(owners[None, :] == devices[:, None], axis=1).astype(I32)
        slabs = decode_sorted(order, sent, jnp.cumsum(sent) - sent, anchors, by_token, scales)
        arrived = lax.all_to_all(slabs, "pool", split_axis=0, concat_axis=0, tiled=True)
        taken = jnp.any((page_owner == position).reshape(16, number), axis=1).astype(I32)
        return assemble(taken, jnp.cumsum(taken) - taken, arrived, number)

    needed = plan[2, 0]
    branch = (needed > ROUNDS).astype(I32) + (needed > LIMIT).astype(I32)
    cache = lax.switch(branch, (in_time, late, padded), cache)
    return (cache, attention)


def decode_pages(anchors, deltas, scales):
    block_scale = jnp.repeat(scales, HD, axis=1)
    rebuilt = anchors[:, None, :].astype(jnp.float32) + block_scale[:, None, :] * deltas.astype(
        jnp.float32
    )
    return jnp.concatenate([anchors[:, None, :], rebuilt.astype(jnp.bfloat16)], axis=1)


def page_scores(work_pages, queries, requests):
    number = work_pages.shape[0]
    key_rows = work_pages[:, :, : KVH * HD].reshape(number, PAGE, KVH, HD)
    picked = jnp.take(queries, requests, axis=0).reshape(number, STEPS, KVH, QH // KVH, HD)
    scores = jnp.einsum(
        "nskgd,ntkd->nskgt", picked, key_rows, preferred_element_type=jnp.float32
    ) * HD ** (-0.5)
    return (scores, jnp.max(scores, axis=4))


def accumulate(scores, page_max, work_pages, requests, shift_max):
    number = work_pages.shape[0]
    rows_out = shift_max.shape[0]
    block_size = min(32, number)
    blocks = number // block_size
    value_rows = work_pages[:, :, KVH * HD :].reshape(blocks, block_size, PAGE, KVH, HD)
    score_blocks = scores.reshape((blocks, block_size) + scores.shape[1:])
    max_blocks = page_max.reshape((blocks, block_size) + page_max.shape[1:])
    request_blocks = requests.reshape(blocks, block_size)

    def block_step(running, pieces):
        totals, numerator = running
        block_scores, block_max, block_values, block_requests = pieces
        exponent = jnp.exp(block_scores - block_max[..., None])
        weights = exponent.astype(jnp.bfloat16)
        page_out = jnp.einsum(
            "nskgt,ntkd->nskgd", weights, block_values, preferred_element_type=jnp.float32
        )
        factor = jnp.exp(block_max - jnp.take(shift_max, block_requests, axis=0))
        select = (block_requests[None, :] == jnp.arange(rows_out, dtype=jnp.int32)[:, None]).astype(
            jnp.float32
        )
        spread = select[:, :, None, None, None] * factor[None]
        totals = totals + jnp.sum(spread * jnp.sum(exponent, axis=4)[None], axis=1)
        numerator = numerator + jnp.einsum(
            "rnskg,nskgd->rskgd", spread, page_out, precision=lax.Precision.HIGHEST
        )
        return ((totals, numerator), None)

    start_totals = jnp.zeros(shift_max.shape, jnp.float32)
    start_numer = jnp.zeros(shift_max.shape + (HD,), jnp.float32)
    finals, ignored = lax.scan(
        block_step,
        (start_totals, start_numer),
        (score_blocks, max_blocks, value_rows, request_blocks),
    )
    return finals


def request_of(index, request_ends):
    return jnp.sum((index[:, None] >= request_ends[None, :]).astype(jnp.int32), axis=1)


def local(anchors, deltas, scales, queries, lengths, page_owner):
    devices = lax.axis_size("pool")
    position = lax.axis_index("pool")
    number = anchors.shape[0]
    capacity = max(2, 2 * number // devices)
    pages = decode_pages(anchors, deltas, scales)
    request_ends = jnp.cumsum(lengths)
    owners = lax.dynamic_slice_in_dim(page_owner, position * number, number, 0)
    marked = (owners[:, None] == jnp.arange(devices, dtype=jnp.int32)[None, :]).astype(jnp.int32)
    ranking = jnp.sum((jnp.cumsum(marked, axis=0) - 1) * marked, axis=1)
    slot_ids = owners * capacity + ranking
    matches = slot_ids[None, :] == jnp.arange(devices * capacity, dtype=jnp.int32)[:, None]
    sources = jnp.sum(jnp.where(matches, jnp.arange(number, dtype=jnp.int32)[None, :], 0), axis=1)
    outgoing = jnp.take(pages, sources, axis=0)
    arrived = lax.all_to_all(outgoing, "pool", split_axis=0, concat_axis=0, tiled=True)
    held_pages = jnp.nonzero(page_owner == position, size=number)[0].astype(jnp.int32)
    senders = held_pages // number
    before = jnp.sum((held_pages[None, :] < (senders * number)[:, None]).astype(jnp.int32), axis=1)
    row_ids = senders * capacity + jnp.arange(number, dtype=jnp.int32) - before
    cache = jnp.take(arrived, row_ids, axis=0)
    columns = QH * HD // devices
    requests = request_of(held_pages, request_ends)
    scores, page_max = page_scores(cache, queries, requests)
    onehot = requests[None, :] == jnp.arange(REQS, dtype=jnp.int32)[:, None]
    local_max = jnp.max(jnp.where(onehot[:, :, None, None, None], page_max[None], -1e30), axis=1)
    global_max = lax.pmax(local_max.astype(jnp.bfloat16), "pool").astype(local_max.dtype)
    totals, numerator = accumulate(scores, page_max, cache, requests, global_max)
    summed, numerator = lax.psum((totals, numerator), "pool")
    whole = (numerator / summed[..., None]).reshape(REQS, STEPS, QH * HD)
    result = lax.dynamic_slice_in_dim(whole, position * columns, columns, 2)
    return (cache, result.astype(jnp.bfloat16))


def solution(mesh):
    placed = (
        P(("groups", "pool"), None),
        P(("groups", "pool"), None, None),
        P(("groups", "pool"), None),
        P("groups", None, None),
        P("groups"),
        P("groups"),
    )
    lanes = mesh.shape["pool"] == 16
    return jax.shard_map(
        local_lanes if lanes else local,
        mesh=mesh,
        in_specs=placed,
        out_specs=(P(("groups", "pool"), None, None), P("groups", None, "pool")),
        check_vma=False,
    )
```

profile of v0, /device:TPU:11, one launch (start us, length us, event | category | flops | bytes accessed | tf_op | source)
XLA Modules:
  0.0 153.7 jit_solution(11723607366192440774)
XLA Ops:
  0.6 0.1 pad_add_fusion.place
  0.7 7.7 %decode_halves.1 = (bf16[64,16,1024]{2,1,0:T(8,128)(2,1)}, bf16[64,16,1024]{2,1,0:T(8,128)(2,1)S(1)}) custom-call(s32[2]{0:T(128)S(1)} %pad_add_fusion.place, s32[16,128]{1,0:T(8,128)} %bitcast.27, bf16[128,1024]{1,0:T(8,128)(2,1)} %val_anchor.7, bf16[15,128,1024]{2,1,0:T(8,128)(2,1)} %bitcast.12, f32[8,128]{1,0:T(8,128)} %bitcast.22), custom_call_target="tpu_custom_call" | custom-call | tf_op jit(solution)/shard_map/decode_halves/pallas_call | solution.py:475
  8.5 0.7 collective-permute-start.4
  9.2 4.3 %make_plan.1.plan.refs_2_.requests.after = s32[8,128]{1,0:T(8,128)S(1)} custom-call(s32[2]{0:T(128)S(1)} %pad_add_fusion.place, s32[16]{0:T(128)} %lengths.1, s32[16,128]{1,0:T(8,128)S(1)} %bitcast.28), custom_call_target="tpu_custom_call" | custom-call | tf_op jit(solution)/shard_map/make_plan/pallas_call | solution.py:401
  13.5 0.0 copy-start.36
  13.5 2.4 %pick_0.1 = (bf16[16,16,1024]{2,1,0:T(8,128)(2,1)S(1)}, bf16[16,16,1024]{2,1,0:T(8,128)(2,1)S(1)}, bf16[24,16,1024]{2,1,0:T(8,128)(2,1)S(1)}) custom-call(s32[8,128]{1,0:T(8,128)S(1)} %make_plan.1.plan.refs_2_.requests.after, s32[2]{0:T(128)S(1)} %pad_add_fusion.place, bf16[64,16,1024]{2,1,0:T(8,128)(2,1)} %get-tuple-element.141.refs_0_, ...), custom_call_target="tpu_custom_call" | custom-call | tf_op jit(solution)/shard_map/pick_0/pallas_call | solution.py:560
  15.9 3.2 %collective-permute-start.5 = (bf16[16,16,1024]{2,1,0:T(8,128)(2,1)S(1)}, bf16[16,16,1024]{2,1,0:T(8,128)(2,1)S(1)}, u32[]{:S(2)}, u32[]{:S(2)}) collective-permute-start(bf16[16,16,1024]{2,1,0:T(8,128)(2,1)S(1)} %get-tuple-element.143.refs_2_), channel_id=1, source_target_pairs={{0,4},{1,5},{2,6},{3,7},{4,8},{5,9},{6,10},{7,11},{8,12},{9,13},{1... | collective-permute-start | bytes 1572872 | tf_op jit(solution)/shard_map/ppermute | solution.py:684
  19.1 2.1 %collective-permute-start.6 = (bf16[16,16,1024]{2,1,0:T(8,128)(2,1)S(1)}, bf16[16,16,1024]{2,1,0:T(8,128)(2,1)S(1)}, u32[]{:S(2)}, u32[]{:S(2)}) collective-permute-start(bf16[16,16,1024]{2,1,0:T(8,128)(2,1)S(1)} %get-tuple-element.144), channel_id=1, source_target_pairs={{4,0},{5,1},{6,2},{7,3},{8,4},{9,5},{10,6},{11,7},{12,8},{13,9},{1... | collective-permute-start | bytes 1572872 | tf_op jit(solution)/shard_map/ppermute | solution.py:684
  21.3 0.3 collective-permute-start.7
  21.6 1.9 %pick_1.1 = (bf16[16,16,1024]{2,1,0:T(8,128)(2,1)S(1)}, bf16[16,16,1024]{2,1,0:T(8,128)(2,1)S(1)}) custom-call(s32[8,128]{1,0:T(8,128)S(1)} %make_plan.1.plan.refs_2_.requests.after, s32[2]{0:T(128)S(1)} %pad_add_fusion.place, bf16[64,16,1024]{2,1,0:T(8,128)(2,1)} %get-tuple-element.141.refs_0_, bf16[64,16,1024]{2,1,0:T(8,128)(2,1)} %collective-permute-done.4.refs_1_, ...), custom_call_target="tpu_custom_call" | custom-call | tf_op jit(solution)/shard_map/pick_1/pallas_call | solution.py:560
  23.4 3.0 %collective-permute-start.8 = (bf16[16,16,1024]{2,1,0:T(8,128)(2,1)S(1)}, bf16[16,16,1024]{2,1,0:T(8,128)(2,1)S(1)}, u32[]{:S(2)}, u32[]{:S(2)}) collective-permute-start(bf16[16,16,1024]{2,1,0:T(8,128)(2,1)S(1)} %get-tuple-element.146), channel_id=1, source_target_pairs={{0,4},{1,5},{2,6},{3,7},{4,8},{5,9},{6,10},{7,11},{8,12},{9,13},{1... | collective-permute-start | bytes 1572872 | tf_op jit(solution)/shard_map/ppermute | solution.py:684
  26.5 2.3 %collective-permute-start.9 = (bf16[16,16,1024]{2,1,0:T(8,128)(2,1)S(1)}, bf16[16,16,1024]{2,1,0:T(8,128)(2,1)S(1)}, u32[]{:S(2)}, u32[]{:S(2)}) collective-permute-start(bf16[16,16,1024]{2,1,0:T(8,128)(2,1)S(1)} %get-tuple-element.147), channel_id=1, source_target_pairs={{4,0},{5,1},{6,2},{7,3},{8,4},{9,5},{10,6},{11,7},{12,8},{13,9},{1... | collective-permute-start | bytes 1572872 | tf_op jit(solution)/shard_map/ppermute | solution.py:684
  28.8 3.4 %attend_0.1.refs_4_.after = bf16[16,112,128]{2,1,0:T(8,128)(2,1)} custom-call(s32[8,128]{1,0:T(8,128)S(1)} %make_plan.1.plan.refs_2_.requests.after, s32[8,128]{1,0:T(8,128)S(1)} %make_plan.1.plan.refs_2_.requests.after, bf16[16,8,8192]{2,1,0:T(8,128)(2,1)S(1)} %copy-done, bf16[16,8,8192]{2,1,0:T(8,128)(2,1)S(1)} %copy-done, ...), custom_call_target="tpu_custom_call" | custom-call | tf_op jit(solution)/shard_map/attend_0/pallas_call | solution.py:136
  32.2 2.1 %collective-permute-done.6.refs_3_ = bf16[16,16,1024]{2,1,0:T(8,128)(2,1)S(1)} collective-permute-done((bf16[16,16,1024]{2,1,0:T(8,128)(2,1)S(1)}, bf16[16,16,1024]{2,1,0:T(8,128)(2,1)S(1)}, u32[]{:S(2)}, u32[]{:S(2)}) %collective-permute-start.6) | collective-permute-done | bytes 524320 | tf_op jit(solution)/shard_map/ppermute | solution.py:684
  34.3 1.8 %pick_2.1 = (bf16[16,16,1024]{2,1,0:T(8,128)(2,1)S(1)}, bf16[16,16,1024]{2,1,0:T(8,128)(2,1)S(1)}, bf16[24,16,1024]{2,1,0:T(8,128)(2,1)S(1)}) custom-call(s32[8,128]{1,0:T(8,128)S(1)} %make_plan.1.plan.refs_2_.requests.after, s32[2]{0:T(128)S(1)} %pad_add_fusion.place, bf16[64,16,1024]{2,1,0:T(8,128)(2,1)} %get-tuple-element.141.refs_0_, ...), custom_call_target="tpu_custom_call" | custom-call | tf_op jit(solution)/shard_map/pick_2/pallas_call | solution.py:560
  36.1 3.2 %collective-permute-start.10 = (bf16[16,16,1024]{2,1,0:T(8,128)(2,1)S(1)}, bf16[16,16,1024]{2,1,0:T(8,128)(2,1)S(1)}, u32[]{:S(2)}, u32[]{:S(2)}) collective-permute-start(bf16[16,16,1024]{2,1,0:T(8,128)(2,1)S(1)} %get-tuple-element.149), channel_id=1, source_target_pairs={{0,4},{1,5},{2,6},{3,7},{4,8},{5,9},{6,10},{7,11},{8,12},{9,13},{1... | collective-permute-start | bytes 1572872 | tf_op jit(solution)/shard_map/ppermute | solution.py:684
  39.2 2.1 %collective-permute-start.11 = (bf16[16,16,1024]{2,1,0:T(8,128)(2,1)S(1)}, bf16[16,16,1024]{2,1,0:T(8,128)(2,1)S(1)}, u32[]{:S(2)}, u32[]{:S(2)}) collective-permute-start(bf16[16,16,1024]{2,1,0:T(8,128)(2,1)S(1)} %get-tuple-element.150), channel_id=1, source_target_pairs={{4,0},{5,1},{6,2},{7,3},{8,4},{9,5},{10,6},{11,7},{12,8},{13,9},{1... | collective-permute-start | bytes 1572872 | tf_op jit(solution)/shard_map/ppermute | solution.py:684
  41.4 1.2 collective-permute-done.8.refs_5_
  42.6 0.2 collective-permute-start.12
  42.9 3.4 %attend_1.1.refs_7_.after = bf16[16,112,128]{2,1,0:T(8,128)(2,1)} custom-call(s32[8,128]{1,0:T(8,128)S(1)} %make_plan.1.plan.refs_2_.requests.after, s32[8,128]{1,0:T(8,128)S(1)} %make_plan.1.plan.refs_2_.requests.after, bf16[16,8,8192]{2,1,0:T(8,128)(2,1)S(1)} %copy-done, bf16[16,8,8192]{2,1,0:T(8,128)(2,1)S(1)} %copy-done, ...), custom_call_target="tpu_custom_call", output_to_operand_aliasing={{}: (10, {})} | custom-call | tf_op jit(solution)/shard_map/attend_1/pallas_call | solution.py:136
  46.2 0.8 pick_3.1
  47.1 3.2 %collective-permute-start.13 = (bf16[16,16,1024]{2,1,0:T(8,128)(2,1)S(1)}, bf16[16,16,1024]{2,1,0:T(8,128)(2,1)S(1)}, u32[]{:S(2)}, u32[]{:S(2)}) collective-permute-start(bf16[16,16,1024]{2,1,0:T(8,128)(2,1)S(1)} %get-tuple-element.153), channel_id=1, source_target_pairs={{0,4},{1,5},{2,6},{3,7},{4,8},{5,9},{6,10},{7,11},{8,12},{9,13},{1... | collective-permute-start | bytes 1572872 | tf_op jit(solution)/shard_map/ppermute | solution.py:684
  50.3 2.1 %collective-permute-start.14 = (bf16[16,16,1024]{2,1,0:T(8,128)(2,1)S(1)}, bf16[16,16,1024]{2,1,0:T(8,128)(2,1)}, u32[]{:S(2)}, u32[]{:S(2)}) collective-permute-start(bf16[16,16,1024]{2,1,0:T(8,128)(2,1)S(1)} %get-tuple-element.154), channel_id=1, source_target_pairs={{4,0},{5,1},{6,2},{7,3},{8,4},{9,5},{10,6},{11,7},{12,8},{13,9},{1... | collective-permute-start | bytes 1572872 | tf_op jit(solution)/shard_map/ppermute | solution.py:684
  52.4 3.4 %attend_2.1.refs_9_.after = bf16[16,112,128]{2,1,0:T(8,128)(2,1)} custom-call(s32[8,128]{1,0:T(8,128)S(1)} %make_plan.1.plan.refs_2_.requests.after, s32[8,128]{1,0:T(8,128)S(1)} %make_plan.1.plan.refs_2_.requests.after, bf16[16,8,8192]{2,1,0:T(8,128)(2,1)S(1)} %copy-done, bf16[16,8,8192]{2,1,0:T(8,128)(2,1)S(1)} %copy-done, ...), custom_call_target="tpu_custom_call", output_to_operand_aliasing={{}: (10, {})} | custom-call | tf_op jit(solution)/shard_map/attend_2/pallas_call | solution.py:136
  55.8 0.9 collective-permute-done.11.refs_8_
  56.7 1.0 pick_4.1
  57.7 3.1 %collective-permute-start.15 = (bf16[16,16,1024]{2,1,0:T(8,128)(2,1)S(1)}, bf16[16,16,1024]{2,1,0:T(8,128)(2,1)}, u32[]{:S(2)}, u32[]{:S(2)}) collective-permute-start(bf16[16,16,1024]{2,1,0:T(8,128)(2,1)S(1)} %get-tuple-element.156), channel_id=1, source_target_pairs={{0,4},{1,5},{2,6},{3,7},{4,8},{5,9},{6,10},{7,11},{8,12},{9,13},{1... | collective-permute-start | bytes 1572872 | tf_op jit(solution)/shard_map/ppermute | solution.py:684
  60.8 3.2 %collective-permute-start.16 = (bf16[16,16,1024]{2,1,0:T(8,128)(2,1)S(1)}, bf16[16,16,1024]{2,1,0:T(8,128)(2,1)}, u32[]{:S(2)}, u32[]{:S(2)}) collective-permute-start(bf16[16,16,1024]{2,1,0:T(8,128)(2,1)S(1)} %get-tuple-element.157), channel_id=1, source_target_pairs={{4,0},{5,1},{6,2},{7,3},{8,4},{9,5},{10,6},{11,7},{12,8},{13,9},{1... | collective-permute-start | bytes 1572872 | tf_op jit(solution)/shard_map/ppermute | solution.py:684
  64.0 1.1 collective-permute-done.13.refs_10_
  65.2 0.8 collective-permute-start.17
  65.9 4.0 %attend_3.1.refs_12_ = bf16[16,112,128]{2,1,0:T(8,128)(2,1)} custom-call(s32[8,128]{1,0:T(8,128)S(1)} %make_plan.1.plan.refs_2_.requests.after, s32[8,128]{1,0:T(8,128)S(1)} %make_plan.1.plan.refs_2_.requests.after, bf16[16,8,8192]{2,1,0:T(8,128)(2,1)S(1)} %copy-done, bf16[16,8,8192]{2,1,0:T(8,128)(2,1)S(1)} %copy-done, ...), custom_call_target="tpu_custom_call", output_to_operand_aliasing={{}: (10, {})} | custom-call | tf_op jit(solution)/shard_map/attend_3/pallas_call | solution.py:136
  70.0 1.9 %pick_5.1 = (bf16[16,16,1024]{2,1,0:T(8,128)(2,1)S(1)}, bf16[16,16,1024]{2,1,0:T(8,128)(2,1)S(1)}) custom-call(s32[8,128]{1,0:T(8,128)S(1)} %make_plan.1.plan.refs_2_.requests.after, s32[2]{0:T(128)S(1)} %pad_add_fusion.place, bf16[64,16,1024]{2,1,0:T(8,128)(2,1)} %get-tuple-element.141.refs_0_, bf16[64,16,1024]{2,1,0:T(8,128)(2,1)} %collective-permute-done.4.refs_1_, ...), custom_call_target="tpu_custom_call" | custom-call | tf_op jit(solution)/shard_map/pick_5/pallas_call | solution.py:560
  71.9 2.9 %collective-permute-start.18 = (bf16[16,16,1024]{2,1,0:T(8,128)(2,1)S(1)}, bf16[16,16,1024]{2,1,0:T(8,128)(2,1)S(1)}, u32[]{:S(2)}, u32[]{:S(2)}) collective-permute-start(bf16[16,16,1024]{2,1,0:T(8,128)(2,1)S(1)} %get-tuple-element.160.refs_14_), channel_id=1, source_target_pairs={{0,4},{1,5},{2,6},{3,7},{4,8},{5,9},{6,10},{7,11},{8,12},{9,13},{1... | collective-permute-start | bytes 1572872 | tf_op jit(solution)/shard_map/ppermute | solution.py:684
  74.8 2.6 %collective-permute-start.19 = (bf16[16,16,1024]{2,1,0:T(8,128)(2,1)S(1)}, bf16[16,16,1024]{2,1,0:T(8,128)(2,1)S(1)}, u32[]{:S(2)}, u32[]{:S(2)}) collective-permute-start(bf16[16,16,1024]{2,1,0:T(8,128)(2,1)S(1)} %get-tuple-element.161), channel_id=1, source_target_pairs={{4,0},{5,1},{6,2},{7,3},{8,4},{9,5},{10,6},{11,7},{12,8},{13,9},{1... | collective-permute-start | bytes 1572872 | tf_op jit(solution)/shard_map/ppermute | solution.py:684
  77.4 1.9 %collective-permute-done.16.refs_13_ = bf16[16,16,1024]{2,1,0:T(8,128)(2,1)} collective-permute-done((bf16[16,16,1024]{2,1,0:T(8,128)(2,1)S(1)}, bf16[16,16,1024]{2,1,0:T(8,128)(2,1)}, u32[]{:S(2)}, u32[]{:S(2)}) %collective-permute-start.16) | collective-permute-done | bytes 524320 | tf_op jit(solution)/shard_map/ppermute | solution.py:684
  79.3 2.0 %pick_6.1 = (bf16[16,16,1024]{2,1,0:T(8,128)(2,1)S(1)}, bf16[16,16,1024]{2,1,0:T(8,128)(2,1)S(1)}, bf16[16,16,1024]{2,1,0:T(8,128)(2,1)S(1)}) custom-call(s32[8,128]{1,0:T(8,128)S(1)} %make_plan.1.plan.refs_2_.requests.after, s32[2]{0:T(128)S(1)} %pad_add_fusion.place, bf16[64,16,1024]{2,1,0:T(8,128)(2,1)} %get-tuple-element.141.refs_0_, ...), custom_call_target="tpu_custom_call" | custom-call | tf_op jit(solution)/shard_map/pick_6/pallas_call | solution.py:560
  81.3 3.0 %collective-permute-start.20 = (bf16[16,16,1024]{2,1,0:T(8,128)(2,1)S(1)}, bf16[16,16,1024]{2,1,0:T(8,128)(2,1)S(1)}, u32[]{:S(2)}, u32[]{:S(2)}) collective-permute-start(bf16[16,16,1024]{2,1,0:T(8,128)(2,1)S(1)} %get-tuple-element.162.refs_17_), channel_id=1, source_target_pairs={{0,4},{1,5},{2,6},{3,7},{4,8},{5,9},{6,10},{7,11},{8,12},{9,13},{1... | collective-permute-start | bytes 1572872 | tf_op jit(solution)/shard_map/ppermute | solution.py:684
  84.4 2.3 %collective-permute-start.21 = (bf16[16,16,1024]{2,1,0:T(8,128)(2,1)S(1)}, bf16[16,16,1024]{2,1,0:T(8,128)(2,1)S(1)}, u32[]{:S(2)}, u32[]{:S(2)}) collective-permute-start(bf16[16,16,1024]{2,1,0:T(8,128)(2,1)S(1)} %get-tuple-element.163), channel_id=1, source_target_pairs={{4,0},{5,1},{6,2},{7,3},{8,4},{9,5},{10,6},{11,7},{12,8},{13,9},{1... | collective-permute-start | bytes 1572872 | tf_op jit(solution)/shard_map/ppermute | solution.py:684
  86.7 0.1 collective-permute-start.25
  86.8 1.0 collective-permute-done.19.refs_16_
  87.8 1.7 %pick_7.1 = (bf16[16,16,1024]{2,1,0:T(8,128)(2,1)S(1)}, bf16[16,16,1024]{2,1,0:T(8,128)(2,1)S(1)}, bf16[16,16,1024]{2,1,0:T(8,128)(2,1)S(1)}) custom-call(s32[8,128]{1,0:T(8,128)S(1)} %make_plan.1.plan.refs_2_.requests.after, s32[2]{0:T(128)S(1)} %pad_add_fusion.place, bf16[64,16,1024]{2,1,0:T(8,128)(2,1)} %get-tuple-element.141.refs_0_, ...), custom_call_target="tpu_custom_call" | custom-call | tf_op jit(solution)/shard_map/pick_7/pallas_call | solution.py:560
  89.6 7.8 %collective-permute-done.20.refs_17_ = bf16[16,16,1024]{2,1,0:T(8,128)(2,1)S(1)} collective-permute-done((bf16[16,16,1024]{2,1,0:T(8,128)(2,1)S(1)}, bf16[16,16,1024]{2,1,0:T(8,128)(2,1)S(1)}, u32[]{:S(2)}, u32[]{:S(2)}) %collective-permute-start.20) | collective-permute-done | bytes 524320 | tf_op jit(solution)/shard_map/ppermute | solution.py:684
  97.4 3.0 %collective-permute-done.21.refs_18_ = bf16[16,16,1024]{2,1,0:T(8,128)(2,1)S(1)} collective-permute-done((bf16[16,16,1024]{2,1,0:T(8,128)(2,1)S(1)}, bf16[16,16,1024]{2,1,0:T(8,128)(2,1)S(1)}, u32[]{:S(2)}, u32[]{:S(2)}) %collective-permute-start.21) | collective-permute-done | bytes 524320 | tf_op jit(solution)/shard_map/ppermute | solution.py:684
  100.4 2.4 %pick_8.1 = (bf16[16,16,1024]{2,1,0:T(8,128)(2,1)S(1)}, bf16[16,16,1024]{2,1,0:T(8,128)(2,1)}, bf16[8,16,1024]{2,1,0:T(8,128)(2,1)S(1)}) custom-call(s32[8,128]{1,0:T(8,128)S(1)} %make_plan.1.plan.refs_2_.requests.after, s32[2]{0:T(128)S(1)} %pad_add_fusion.place, bf16[64,16,1024]{2,1,0:T(8,128)(2,1)} %get-tuple-element.141.refs_0_, ...), custom_call_target="tpu_custom_call" | custom-call | tf_op jit(solution)/shard_map/pick_8/pallas_call | solution.py:560
  102.9 7.6 %all-to-all-start.1 = ((bf16[16,112,128]{2,1,0:T(8,128)(2,1)}), bf16[16,112,128]{2,1,0:T(8,128)(2,1)S(1)}, u32[]{:S(2)}, u32[]{:S(2)}) async-start(bf16[16,112,128]{2,1,0:T(8,128)(2,1)} %attend_3.1.refs_12_), calls=%async_computation.1 | async-start | bytes 917504 | tf_op jit(solution)/shard_map/all_to_all | solution.py:725
  110.6 3.1 %collective-permute-start.26 = (bf16[16,16,1024]{2,1,0:T(8,128)(2,1)S(1)}, bf16[16,16,1024]{2,1,0:T(8,128)(2,1)S(1)}, u32[]{:S(2)}, u32[]{:S(2)}) collective-permute-start(bf16[16,16,1024]{2,1,0:T(8,128)(2,1)S(1)} %get-tuple-element.164.refs_19_), channel_id=1, source_target_pairs={{0,4},{1,5},{2,6},{3,7},{4,8},{5,9},{6,10},{7,11},{8,12},{9,13},{1... | collective-permute-start | bytes 1572872 | tf_op jit(solution)/shard_map/ppermute | solution.py:684
  113.6 2.2 %collective-permute-start.27 = (bf16[16,16,1024]{2,1,0:T(8,128)(2,1)S(1)}, bf16[16,16,1024]{2,1,0:T(8,128)(2,1)S(1)}, u32[]{:S(2)}, u32[]{:S(2)}) collective-permute-start(bf16[16,16,1024]{2,1,0:T(8,128)(2,1)S(1)} %get-tuple-element.169), channel_id=1, source_target_pairs={{4,0},{5,1},{6,2},{7,3},{8,4},{9,5},{10,6},{11,7},{12,8},{13,9},{1... | collective-permute-start | bytes 1572872 | tf_op jit(solution)/shard_map/ppermute | solution.py:684
  115.9 0.3 collective-permute-start.28
  116.2 3.1 %collective-permute-start.22 = (bf16[16,16,1024]{2,1,0:T(8,128)(2,1)S(1)}, bf16[16,16,1024]{2,1,0:T(8,128)(2,1)}, u32[]{:S(2)}, u32[]{:S(2)}) collective-permute-start(bf16[16,16,1024]{2,1,0:T(8,128)(2,1)S(1)} %get-tuple-element.165.refs_23_.after), channel_id=1, source_target_pairs={{0,4},{1,5},{2,6},{3,7},{4,8},{5,9},{6,10},{7,11},{8,12},{9,13},{1... | collective-permute-start | bytes 1572872 | tf_op jit(solution)/shard_map/ppermute | solution.py:684
  119.3 3.0 %collective-permute-start.23 = (bf16[16,16,1024]{2,1,0:T(8,128)(2,1)}, bf16[16,16,1024]{2,1,0:T(8,128)(2,1)}, u32[]{:S(2)}, u32[]{:S(2)}) collective-permute-start(bf16[16,16,1024]{2,1,0:T(8,128)(2,1)} %get-tuple-element.166), channel_id=1, source_target_pairs={{4,0},{5,1},{6,2},{7,3},{8,4},{9,5},{10,6},{11,7},{12,8},{13,9},{1... | collective-permute-start | bytes 1572872 | tf_op jit(solution)/shard_map/ppermute | solution.py:684
  122.3 9.7 %collective-permute-done.26.refs_20_ = bf16[16,16,1024]{2,1,0:T(8,128)(2,1)S(1)} collective-permute-done((bf16[16,16,1024]{2,1,0:T(8,128)(2,1)S(1)}, bf16[16,16,1024]{2,1,0:T(8,128)(2,1)S(1)}, u32[]{:S(2)}, u32[]{:S(2)}) %collective-permute-start.26) | collective-permute-done | bytes 524320 | tf_op jit(solution)/shard_map/ppermute | solution.py:684
  132.1 0.3 collective-permute-start.24
  132.4 1.5 collective-permute-done.27.refs_21_
  133.9 2.8 %gather_give.4.refs_6_ = bf16[64,16,1024]{2,1,0:T(8,128)(2,1)S(1)} custom-call(s32[8,128]{1,0:T(8,128)S(1)} %make_plan.1.plan.refs_2_.requests.after, s32[2]{0:T(128)S(1)} %pad_add_fusion.place, bf16[64,16,1024]{2,1,0:T(8,128)(2,1)} %get-tuple-element.141.refs_0_, bf16[64,16,1024]{2,1,0:T(8,128)(2,1)} %collective-permute-done.4.refs_1_, ...), custom_call_target="tpu_custom_call" | custom-call | tf_op jit(solution)/shard_map/gather_give/pallas_call | solution.py:614
  136.9 3.3 %gather_own.4.refs_5_.refs_6_ = bf16[128,16,1024]{2,1,0:T(8,128)(2,1)} custom-call(s32[8,128]{1,0:T(8,128)S(1)} %make_plan.1.plan.refs_2_.requests.after, s32[2]{0:T(128)S(1)} %pad_add_fusion.place, bf16[64,16,1024]{2,1,0:T(8,128)(2,1)} %get-tuple-element.141.refs_0_, bf16[64,16,1024]{2,1,0:T(8,128)(2,1)} %collective-permute-done.4.refs_1_, ...), custom_call_target="tpu_custom_call" | custom-call | tf_op jit(solution)/shard_map/gather_own/pallas_call | solution.py:614
  140.2 1.8 %merge.1 = bf16[16,8,512]{2,1,0:T(8,128)(2,1)} custom-call(s32[8,128]{1,0:T(8,128)S(1)} %make_plan.1.plan.refs_2_.requests.after, s32[2]{0:T(128)S(1)} %pad_add_fusion.place, bf16[16,112,128]{2,1,0:T(8,128)(2,1)S(1)} %all-to-all-done.1.parts, bf16[16,16,1024]{2,1,0:T(8,128)(2,1)S(1)} %get-tuple-element.165.refs_23_.after), custom_call_target="tpu_custom_call" | custom-call | tf_op jit(solution)/shard_map/merge/pallas_call | solution.py:202
  142.0 1.2 collective-permute-done.22.refs_2_
  143.2 1.9 %collective-permute-done.23.refs_3_ = bf16[16,16,1024]{2,1,0:T(8,128)(2,1)} collective-permute-done((bf16[16,16,1024]{2,1,0:T(8,128)(2,1)}, bf16[16,16,1024]{2,1,0:T(8,128)(2,1)}, u32[]{:S(2)}, u32[]{:S(2)}) %collective-permute-start.23) | collective-permute-done | bytes 524320 | tf_op jit(solution)/shard_map/ppermute | solution.py:684
  145.1 2.0 %gather_give.5.refs_5_ = bf16[64,16,1024]{2,1,0:T(8,128)(2,1)S(1)} custom-call(s32[8,128]{1,0:T(8,128)S(1)} %make_plan.1.plan.refs_2_.requests.after, s32[2]{0:T(128)S(1)} %pad_add_fusion.place, bf16[64,16,1024]{2,1,0:T(8,128)(2,1)} %get-tuple-element.141.refs_0_, ...), custom_call_target="tpu_custom_call", output_to_operand_aliasing={{}: (8, {})} | custom-call | tf_op jit(solution)/shard_map/gather_give/pallas_call | solution.py:614
  147.1 0.2 collective-permute-start.29
  147.3 0.5 slice.3
  149.1 1.2 gather_own.5.cache
  150.3 1.1 collective-permute-done.29.other
  151.4 2.1 %fill.3 = bf16[128,16,1024]{2,1,0:T(8,128)(2,1)} custom-call(s32[2]{0:T(128)S(1)} %pad_add_fusion.place, bf16[128,16,1024]{2,1,0:T(8,128)(2,1)} %gather_own.5.cache, bf16[64,16,1024]{2,1,0:T(8,128)(2,1)S(1)} %collective-permute-done.29.other), custom_call_target="tpu_custom_call", output_to_operand_aliasing={{}: (1, {})} | custom-call | tf_op jit(solution)/shard_map/fill/pallas_call | solution.py:655
  (106 shorter events, 0.2 us)
Async XLA Ops:
  0.6 8.6 %copy-start.59 = (s32[2048]{0:T(1024)S(1)}, s32[2048]{0:T(1024)}, u32[]{:S(2)}) copy-start(s32[2048]{0:T(1024)} %param.14) | copy-start | bytes 24580
  8.5 5.0 %collective-permute-start.4 = (bf16[64,16,1024]{2,1,0:T(8,128)(2,1)S(1)}, bf16[64,16,1024]{2,1,0:T(8,128)(2,1)}, u32[]{:S(2)}, u32[]{:S(2)}) collective-permute-start(bf16[64,16,1024]{2,1,0:T(8,128)(2,1)S(1)} %get-tuple-element.142), channel_id=1, source_target_pairs={{0,1},{1,0},{2,3},{3,2},{4,5},{5,4},{6,7},{7,6},{8,9},{9,8},{10,11... | collective-permute-start | bytes 6291464 | tf_op jit(solution)/shard_map/ppermute | solution.py:712
  13.5 15.3 %copy-start = (bf16[16,8,8192]{2,1,0:T(8,128)(2,1)S(1)}, bf16[16,8,8192]{2,1,0:T(8,128)(2,1)}, u32[]{:S(2)}) copy-start(bf16[16,8,8192]{2,1,0:T(8,128)(2,1)} %third.7) | copy-start | bytes 6291460
  13.5 15.3 %copy-start.1 = (bf16[128,15,1024]{2,0,1:T(8,128)(2,1)S(1)}, bf16[128,15,1024]{2,0,1:T(8,128)(2,1)}, u32[]{:S(2)}) copy-start(bf16[128,15,1024]{2,0,1:T(8,128)(2,1)} %param.10) | copy-start | bytes 11796484
  13.5 15.3 %copy-start.36 = (bf16[128,1024]{1,0:T(8,128)(2,1)S(1)}, bf16[128,1024]{1,0:T(8,128)(2,1)}, u32[]{:S(2)}) copy-start(bf16[128,1024]{1,0:T(8,128)(2,1)} %val_anchor.7) | copy-start | bytes 786436
  13.5 15.3 %copy-start.58 = (f32[128,8]{0,1:T(8,128)S(1)}, f32[128,8]{0,1:T(8,128)}, u32[]{:S(2)}) copy-start(f32[128,8]{0,1:T(8,128)} %param.11) | copy-start | bytes 12292
  15.9 16.2 %collective-permute-start.5 = (bf16[16,16,1024]{2,1,0:T(8,128)(2,1)S(1)}, bf16[16,16,1024]{2,1,0:T(8,128)(2,1)S(1)}, u32[]{:S(2)}, u32[]{:S(2)}) collective-permute-start(bf16[16,16,1024]{2,1,0:T(8,128)(2,1)S(1)} %get-tuple-element.143.refs_2_), channel_id=1, source_target_pairs={{0,4},{1,5},{2,6},{3,7},{4,8},{5,9},{6,10},{7,11},{8,12},{9,13},{1... | collective-permute-start | bytes 1572872 | tf_op jit(solution)/shard_map/ppermute | solution.py:684
  19.1 15.1 %collective-permute-start.6 = (bf16[16,16,1024]{2,1,0:T(8,128)(2,1)S(1)}, bf16[16,16,1024]{2,1,0:T(8,128)(2,1)S(1)}, u32[]{:S(2)}, u32[]{:S(2)}) collective-permute-start(bf16[16,16,1024]{2,1,0:T(8,128)(2,1)S(1)} %get-tuple-element.144), channel_id=1, source_target_pairs={{4,0},{5,1},{6,2},{7,3},{8,4},{9,5},{10,6},{11,7},{12,8},{13,9},{1... | collective-permute-start | bytes 1572872 | tf_op jit(solution)/shard_map/ppermute | solution.py:684
  21.3 25.0 %collective-permute-start.7 = (bf16[24,16,1024]{2,1,0:T(8,128)(2,1)S(1)}, bf16[24,16,1024]{2,1,0:T(8,128)(2,1)S(1)}, u32[]{:S(2)}, u32[]{:S(2)}) collective-permute-start(bf16[24,16,1024]{2,1,0:T(8,128)(2,1)S(1)} %get-tuple-element.145), channel_id=1, source_target_pairs={{0,2},{1,3},{2,0},{3,1},{4,6},{5,7},{6,4},{7,5},{8,10},{9,11},{10,... | collective-permute-start | bytes 2359304 | tf_op jit(solution)/shard_map/ppermute | solution.py:684
  23.4 19.2 %collective-permute-start.8 = (bf16[16,16,1024]{2,1,0:T(8,128)(2,1)S(1)}, bf16[16,16,1024]{2,1,0:T(8,128)(2,1)S(1)}, u32[]{:S(2)}, u32[]{:S(2)}) collective-permute-start(bf16[16,16,1024]{2,1,0:T(8,128)(2,1)S(1)} %get-tuple-element.146), channel_id=1, source_target_pairs={{0,4},{1,5},{2,6},{3,7},{4,8},{5,9},{6,10},{7,11},{8,12},{9,13},{1... | collective-permute-start | bytes 1572872 | tf_op jit(solution)/shard_map/ppermute | solution.py:684
  26.5 19.7 %collective-permute-start.9 = (bf16[16,16,1024]{2,1,0:T(8,128)(2,1)S(1)}, bf16[16,16,1024]{2,1,0:T(8,128)(2,1)S(1)}, u32[]{:S(2)}, u32[]{:S(2)}) collective-permute-start(bf16[16,16,1024]{2,1,0:T(8,128)(2,1)S(1)} %get-tuple-element.147), channel_id=1, source_target_pairs={{4,0},{5,1},{6,2},{7,3},{8,4},{9,5},{10,6},{11,7},{12,8},{13,9},{1... | collective-permute-start | bytes 1572872 | tf_op jit(solution)/shard_map/ppermute | solution.py:684
  32.2 68.2 %copy-start.5 = (bf16[16,16,1024]{2,1,0:T(8,128)(2,1)}, bf16[16,16,1024]{2,1,0:T(8,128)(2,1)S(1)}, u32[]{:S(2)}) copy-start(bf16[16,16,1024]{2,1,0:T(8,128)(2,1)S(1)} %collective-permute-done.5.refs_2_) | copy-start | bytes 1572868
  34.2 66.1 %copy-start.8 = (bf16[16,16,1024]{2,1,0:T(8,128)(2,1)}, bf16[16,16,1024]{2,1,0:T(8,128)(2,1)S(1)}, u32[]{:S(2)}) copy-start(bf16[16,16,1024]{2,1,0:T(8,128)(2,1)S(1)} %collective-permute-done.6.refs_3_) | copy-start | bytes 1572868
  36.1 19.7 %collective-permute-start.10 = (bf16[16,16,1024]{2,1,0:T(8,128)(2,1)S(1)}, bf16[16,16,1024]{2,1,0:T(8,128)(2,1)S(1)}, u32[]{:S(2)}, u32[]{:S(2)}) collective-permute-start(bf16[16,16,1024]{2,1,0:T(8,128)(2,1)S(1)} %get-tuple-element.149), channel_id=1, source_target_pairs={{0,4},{1,5},{2,6},{3,7},{4,8},{5,9},{6,10},{7,11},{8,12},{9,13},{1... | collective-permute-start | bytes 1572872 | tf_op jit(solution)/shard_map/ppermute | solution.py:684
  39.2 17.5 %collective-permute-start.11 = (bf16[16,16,1024]{2,1,0:T(8,128)(2,1)S(1)}, bf16[16,16,1024]{2,1,0:T(8,128)(2,1)S(1)}, u32[]{:S(2)}, u32[]{:S(2)}) collective-permute-start(bf16[16,16,1024]{2,1,0:T(8,128)(2,1)S(1)} %get-tuple-element.150), channel_id=1, source_target_pairs={{4,0},{5,1},{6,2},{7,3},{8,4},{9,5},{10,6},{11,7},{12,8},{13,9},{1... | collective-permute-start | bytes 1572872 | tf_op jit(solution)/shard_map/ppermute | solution.py:684
  42.6 45.2 %copy-start.14 = (bf16[16,16,1024]{2,1,0:T(8,128)(2,1)}, bf16[16,16,1024]{2,1,0:T(8,128)(2,1)S(1)}, u32[]{:S(2)}) copy-start(bf16[16,16,1024]{2,1,0:T(8,128)(2,1)S(1)} %collective-permute-done.8.refs_5_) | copy-start | bytes 1572868
  42.6 27.4 %collective-permute-start.12 = (bf16[24,16,1024]{2,1,0:T(8,128)(2,1)S(1)}, bf16[24,16,1024]{2,1,0:T(8,128)(2,1)S(1)}, u32[]{:S(2)}, u32[]{:S(2)}) collective-permute-start(bf16[24,16,1024]{2,1,0:T(8,128)(2,1)S(1)} %get-tuple-element.151), channel_id=1, source_target_pairs={{0,2},{1,3},{2,0},{3,1},{4,6},{5,7},{6,4},{7,5},{8,10},{9,11},{10,... | collective-permute-start | bytes 2359304 | tf_op jit(solution)/shard_map/ppermute | solution.py:684
  46.2 6.2 %copy-start.37 = (bf16[128,1024]{1,0:T(8,128)(2,1)S(1)}, bf16[128,1024]{1,0:T(8,128)(2,1)}, u32[]{:S(2)}) copy-start(bf16[128,1024]{1,0:T(8,128)(2,1)} %val_anchor.7) | copy-start | bytes 786436
  46.2 33.1 %copy-start.17 = (bf16[16,16,1024]{2,1,0:T(8,128)(2,1)}, bf16[16,16,1024]{2,1,0:T(8,128)(2,1)S(1)}, u32[]{:S(2)}) copy-start(bf16[16,16,1024]{2,1,0:T(8,128)(2,1)S(1)} %collective-permute-done.9.refs_6_) | copy-start | bytes 1572868
  46.2 54.2 %copy-start.2 = (bf16[24,16,1024]{2,1,0:T(8,128)(2,1)}, bf16[24,16,1024]{2,1,0:T(8,128)(2,1)S(1)}, u32[]{:S(2)}) copy-start(bf16[24,16,1024]{2,1,0:T(8,128)(2,1)S(1)} %collective-permute-done.7.refs_4_) | copy-start | bytes 2359300
  47.1 18.1 %collective-permute-start.13 = (bf16[16,16,1024]{2,1,0:T(8,128)(2,1)S(1)}, bf16[16,16,1024]{2,1,0:T(8,128)(2,1)S(1)}, u32[]{:S(2)}, u32[]{:S(2)}) collective-permute-start(bf16[16,16,1024]{2,1,0:T(8,128)(2,1)S(1)} %get-tuple-element.153), channel_id=1, source_target_pairs={{0,4},{1,5},{2,6},{3,7},{4,8},{5,9},{6,10},{7,11},{8,12},{9,13},{1... | collective-permute-start | bytes 1572872 | tf_op jit(solution)/shard_map/ppermute | solution.py:684
  50.3 19.7 %collective-permute-start.14 = (bf16[16,16,1024]{2,1,0:T(8,128)(2,1)S(1)}, bf16[16,16,1024]{2,1,0:T(8,128)(2,1)}, u32[]{:S(2)}, u32[]{:S(2)}) collective-permute-start(bf16[16,16,1024]{2,1,0:T(8,128)(2,1)S(1)} %get-tuple-element.154), channel_id=1, source_target_pairs={{4,0},{5,1},{6,2},{7,3},{8,4},{9,5},{10,6},{11,7},{12,8},{13,9},{1... | collective-permute-start | bytes 1572872 | tf_op jit(solution)/shard_map/ppermute | solution.py:684
  55.8 23.5 %copy-start.21 = (bf16[16,16,1024]{2,1,0:T(8,128)(2,1)}, bf16[16,16,1024]{2,1,0:T(8,128)(2,1)S(1)}, u32[]{:S(2)}) copy-start(bf16[16,16,1024]{2,1,0:T(8,128)(2,1)S(1)} %collective-permute-done.10.refs_7_) | copy-start | bytes 1572868
  56.7 22.6 %copy-start.25 = (bf16[16,16,1024]{2,1,0:T(8,128)(2,1)}, bf16[16,16,1024]{2,1,0:T(8,128)(2,1)S(1)}, u32[]{:S(2)}) copy-start(bf16[16,16,1024]{2,1,0:T(8,128)(2,1)S(1)} %collective-permute-done.11.refs_8_) | copy-start | bytes 1572868
  57.7 19.6 %collective-permute-start.15 = (bf16[16,16,1024]{2,1,0:T(8,128)(2,1)S(1)}, bf16[16,16,1024]{2,1,0:T(8,128)(2,1)}, u32[]{:S(2)}, u32[]{:S(2)}) collective-permute-start(bf16[16,16,1024]{2,1,0:T(8,128)(2,1)S(1)} %get-tuple-element.156), channel_id=1, source_target_pairs={{0,4},{1,5},{2,6},{3,7},{4,8},{5,9},{6,10},{7,11},{8,12},{9,13},{1... | collective-permute-start | bytes 1572872 | tf_op jit(solution)/shard_map/ppermute | solution.py:684
  60.8 18.4 %collective-permute-start.16 = (bf16[16,16,1024]{2,1,0:T(8,128)(2,1)S(1)}, bf16[16,16,1024]{2,1,0:T(8,128)(2,1)}, u32[]{:S(2)}, u32[]{:S(2)}) collective-permute-start(bf16[16,16,1024]{2,1,0:T(8,128)(2,1)S(1)} %get-tuple-element.157), channel_id=1, source_target_pairs={{4,0},{5,1},{6,2},{7,3},{8,4},{9,5},{10,6},{11,7},{12,8},{13,9},{1... | collective-permute-start | bytes 1572872 | tf_op jit(solution)/shard_map/ppermute | solution.py:684
  65.2 4.8 %copy-start.29 = (bf16[16,16,1024]{2,1,0:T(8,128)(2,1)}, bf16[16,16,1024]{2,1,0:T(8,128)(2,1)S(1)}, u32[]{:S(2)}) copy-start(bf16[16,16,1024]{2,1,0:T(8,128)(2,1)S(1)} %collective-permute-done.13.refs_10_) | copy-start | bytes 1572868
  65.2 22.6 %collective-permute-start.17 = (bf16[24,16,1024]{2,1,0:T(8,128)(2,1)S(1)}, bf16[24,16,1024]{2,1,0:T(8,128)(2,1)S(1)}, u32[]{:S(2)}, u32[]{:S(2)}) collective-permute-start(bf16[24,16,1024]{2,1,0:T(8,128)(2,1)S(1)} %get-tuple-element.158), channel_id=1, source_target_pairs={{0,2},{1,3},{2,0},{3,1},{4,6},{5,7},{6,4},{7,5},{8,10},{9,11},{10,... | collective-permute-start | bytes 2359304 | tf_op jit(solution)/shard_map/ppermute | solution.py:684
  70.0 17.8 %copy-start.11 = (bf16[24,16,1024]{2,1,0:T(8,128)(2,1)}, bf16[24,16,1024]{2,1,0:T(8,128)(2,1)S(1)}, u32[]{:S(2)}) copy-start(bf16[24,16,1024]{2,1,0:T(8,128)(2,1)S(1)} %collective-permute-done.12.refs_9_) | copy-start | bytes 2359300
  71.9 14.8 %collective-permute-start.18 = (bf16[16,16,1024]{2,1,0:T(8,128)(2,1)S(1)}, bf16[16,16,1024]{2,1,0:T(8,128)(2,1)S(1)}, u32[]{:S(2)}, u32[]{:S(2)}) collective-permute-start(bf16[16,16,1024]{2,1,0:T(8,128)(2,1)S(1)} %get-tuple-element.160.refs_14_), channel_id=1, source_target_pairs={{0,4},{1,5},{2,6},{3,7},{4,8},{5,9},{6,10},{7,11},{8,12},{9,13},{1... | collective-permute-start | bytes 1572872 | tf_op jit(solution)/shard_map/ppermute | solution.py:684
  74.7 13.1 %copy-start.30 = (bf16[16,16,1024]{2,1,0:T(8,128)(2,1)S(1)}, bf16[16,16,1024]{2,1,0:T(8,128)(2,1)}, u32[]{:S(2)}) copy-start(bf16[16,16,1024]{2,1,0:T(8,128)(2,1)} %copy-done.29) | copy-start | bytes 1572868
  74.8 13.0 %collective-permute-start.19 = (bf16[16,16,1024]{2,1,0:T(8,128)(2,1)S(1)}, bf16[16,16,1024]{2,1,0:T(8,128)(2,1)S(1)}, u32[]{:S(2)}, u32[]{:S(2)}) collective-permute-start(bf16[16,16,1024]{2,1,0:T(8,128)(2,1)S(1)} %get-tuple-element.161), channel_id=1, source_target_pairs={{4,0},{5,1},{6,2},{7,3},{8,4},{9,5},{10,6},{11,7},{12,8},{13,9},{1... | collective-permute-start | bytes 1572872 | tf_op jit(solution)/shard_map/ppermute | solution.py:684
  81.3 16.0 %collective-permute-start.20 = (bf16[16,16,1024]{2,1,0:T(8,128)(2,1)S(1)}, bf16[16,16,1024]{2,1,0:T(8,128)(2,1)S(1)}, u32[]{:S(2)}, u32[]{:S(2)}) collective-permute-start(bf16[16,16,1024]{2,1,0:T(8,128)(2,1)S(1)} %get-tuple-element.162.refs_17_), channel_id=1, source_target_pairs={{0,4},{1,5},{2,6},{3,7},{4,8},{5,9},{6,10},{7,11},{8,12},{9,13},{1... | collective-permute-start | bytes 1572872 | tf_op jit(solution)/shard_map/ppermute | solution.py:684
  84.4 16.0 %collective-permute-start.21 = (bf16[16,16,1024]{2,1,0:T(8,128)(2,1)S(1)}, bf16[16,16,1024]{2,1,0:T(8,128)(2,1)S(1)}, u32[]{:S(2)}, u32[]{:S(2)}) collective-permute-start(bf16[16,16,1024]{2,1,0:T(8,128)(2,1)S(1)} %get-tuple-element.163), channel_id=1, source_target_pairs={{4,0},{5,1},{6,2},{7,3},{8,4},{9,5},{10,6},{11,7},{12,8},{13,9},{1... | collective-permute-start | bytes 1572872 | tf_op jit(solution)/shard_map/ppermute | solution.py:684
  86.7 13.7 %copy-start.38 = (bf16[16,16,1024]{2,1,0:T(8,128)(2,1)}, bf16[16,16,1024]{2,1,0:T(8,128)(2,1)S(1)}, u32[]{:S(2)}) copy-start(bf16[16,16,1024]{2,1,0:T(8,128)(2,1)S(1)} %collective-permute-done.18.refs_15_) | copy-start | bytes 1572868
  86.7 13.7 %copy-start.18 = (bf16[16,16,1024]{2,1,0:T(8,128)(2,1)S(1)}, bf16[16,16,1024]{2,1,0:T(8,128)(2,1)}, u32[]{:S(2)}) copy-start(bf16[16,16,1024]{2,1,0:T(8,128)(2,1)} %copy-done.17) | copy-start | bytes 1572868
  86.7 13.7 %copy-start.22 = (bf16[16,16,1024]{2,1,0:T(8,128)(2,1)S(1)}, bf16[16,16,1024]{2,1,0:T(8,128)(2,1)}, u32[]{:S(2)}) copy-start(bf16[16,16,1024]{2,1,0:T(8,128)(2,1)} %copy-done.21) | copy-start | bytes 1572868
  86.7 13.7 %copy-start.26 = (bf16[16,16,1024]{2,1,0:T(8,128)(2,1)S(1)}, bf16[16,16,1024]{2,1,0:T(8,128)(2,1)}, u32[]{:S(2)}) copy-start(bf16[16,16,1024]{2,1,0:T(8,128)(2,1)} %copy-done.25) | copy-start | bytes 1572868
  86.7 32.6 %collective-permute-start.25 = (bf16[16,16,1024]{2,1,0:T(8,128)(2,1)S(1)}, bf16[16,16,1024]{2,1,0:T(8,128)(2,1)}, u32[]{:S(2)}, u32[]{:S(2)}) collective-permute-start(bf16[16,16,1024]{2,1,0:T(8,128)(2,1)S(1)} %get-tuple-element.168), channel_id=1, source_target_pairs={{0,2},{1,3},{2,0},{3,1},{4,6},{5,7},{6,4},{7,5},{8,10},{9,11},{10,... | collective-permute-start | bytes 1572872 | tf_op jit(solution)/shard_map/ppermute | solution.py:684
  87.8 12.6 %copy-start.41 = (bf16[16,16,1024]{2,1,0:T(8,128)(2,1)}, bf16[16,16,1024]{2,1,0:T(8,128)(2,1)S(1)}, u32[]{:S(2)}) copy-start(bf16[16,16,1024]{2,1,0:T(8,128)(2,1)S(1)} %collective-permute-done.19.refs_16_) | copy-start | bytes 1572868
  87.8 12.6 %copy-start.33 = (bf16[24,16,1024]{2,1,0:T(8,128)(2,1)}, bf16[24,16,1024]{2,1,0:T(8,128)(2,1)S(1)}, u32[]{:S(2)}) copy-start(bf16[24,16,1024]{2,1,0:T(8,128)(2,1)S(1)} %collective-permute-done.17.refs_14_) | copy-start | bytes 2359300
  97.3 5.5 %copy-start.44 = (bf16[16,16,1024]{2,1,0:T(8,128)(2,1)}, bf16[16,16,1024]{2,1,0:T(8,128)(2,1)S(1)}, u32[]{:S(2)}) copy-start(bf16[16,16,1024]{2,1,0:T(8,128)(2,1)S(1)} %collective-permute-done.20.refs_17_) | copy-start | bytes 1572868
  102.9 37.3 %all-to-all-start.1 = ((bf16[16,112,128]{2,1,0:T(8,128)(2,1)}), bf16[16,112,128]{2,1,0:T(8,128)(2,1)S(1)}, u32[]{:S(2)}, u32[]{:S(2)}) async-start(bf16[16,112,128]{2,1,0:T(8,128)(2,1)} %attend_3.1.refs_12_), calls=%async_computation.1 | async-start | bytes 917504 | tf_op jit(solution)/shard_map/all_to_all | solution.py:725
  110.6 21.4 %collective-permute-start.26 = (bf16[16,16,1024]{2,1,0:T(8,128)(2,1)S(1)}, bf16[16,16,1024]{2,1,0:T(8,128)(2,1)S(1)}, u32[]{:S(2)}, u32[]{:S(2)}) collective-permute-start(bf16[16,16,1024]{2,1,0:T(8,128)(2,1)S(1)} %get-tuple-element.164.refs_19_), channel_id=1, source_target_pairs={{0,4},{1,5},{2,6},{3,7},{4,8},{5,9},{6,10},{7,11},{8,12},{9,13},{1... | collective-permute-start | bytes 1572872 | tf_op jit(solution)/shard_map/ppermute | solution.py:684
  113.6 20.2 %collective-permute-start.27 = (bf16[16,16,1024]{2,1,0:T(8,128)(2,1)S(1)}, bf16[16,16,1024]{2,1,0:T(8,128)(2,1)S(1)}, u32[]{:S(2)}, u32[]{:S(2)}) collective-permute-start(bf16[16,16,1024]{2,1,0:T(8,128)(2,1)S(1)} %get-tuple-element.169), channel_id=1, source_target_pairs={{4,0},{5,1},{6,2},{7,3},{8,4},{9,5},{10,6},{11,7},{12,8},{13,9},{1... | collective-permute-start | bytes 1572872 | tf_op jit(solution)/shard_map/ppermute | solution.py:684
  115.9 18.0 %collective-permute-start.28 = (bf16[16,16,1024]{2,1,0:T(8,128)(2,1)S(1)}, bf16[16,16,1024]{2,1,0:T(8,128)(2,1)S(1)}, u32[]{:S(2)}, u32[]{:S(2)}) collective-permute-start(bf16[16,16,1024]{2,1,0:T(8,128)(2,1)S(1)} %get-tuple-element.170), channel_id=1, source_target_pairs={{0,2},{1,3},{2,0},{3,1},{4,6},{5,7},{6,4},{7,5},{8,10},{9,11},{10,... | collective-permute-start | bytes 1572872 | tf_op jit(solution)/shard_map/ppermute | solution.py:684
  116.2 27.0 %collective-permute-start.22 = (bf16[16,16,1024]{2,1,0:T(8,128)(2,1)S(1)}, bf16[16,16,1024]{2,1,0:T(8,128)(2,1)}, u32[]{:S(2)}, u32[]{:S(2)}) collective-permute-start(bf16[16,16,1024]{2,1,0:T(8,128)(2,1)S(1)} %get-tuple-element.165.refs_23_.after), channel_id=1, source_target_pairs={{0,4},{1,5},{2,6},{3,7},{4,8},{5,9},{6,10},{7,11},{8,12},{9,13},{1... | collective-permute-start | bytes 1572872 | tf_op jit(solution)/shard_map/ppermute | solution.py:684
  119.3 25.8 %collective-permute-start.23 = (bf16[16,16,1024]{2,1,0:T(8,128)(2,1)}, bf16[16,16,1024]{2,1,0:T(8,128)(2,1)}, u32[]{:S(2)}, u32[]{:S(2)}) collective-permute-start(bf16[16,16,1024]{2,1,0:T(8,128)(2,1)} %get-tuple-element.166), channel_id=1, source_target_pairs={{4,0},{5,1},{6,2},{7,3},{8,4},{9,5},{10,6},{11,7},{12,8},{13,9},{1... | collective-permute-start | bytes 1572872 | tf_op jit(solution)/shard_map/ppermute | solution.py:684
  132.0 4.8 %copy-start.3 = (bf16[24,16,1024]{2,1,0:T(8,128)(2,1)S(1)}, bf16[24,16,1024]{2,1,0:T(8,128)(2,1)}, u32[]{:S(2)}) copy-start(bf16[24,16,1024]{2,1,0:T(8,128)(2,1)} %copy-done.2) | copy-start | bytes 2359300
  132.0 4.8 %copy-start.6 = (bf16[16,16,1024]{2,1,0:T(8,128)(2,1)S(1)}, bf16[16,16,1024]{2,1,0:T(8,128)(2,1)}, u32[]{:S(2)}) copy-start(bf16[16,16,1024]{2,1,0:T(8,128)(2,1)} %copy-done.5) | copy-start | bytes 1572868
  132.0 4.8 %copy-start.9 = (bf16[16,16,1024]{2,1,0:T(8,128)(2,1)S(1)}, bf16[16,16,1024]{2,1,0:T(8,128)(2,1)}, u32[]{:S(2)}) copy-start(bf16[16,16,1024]{2,1,0:T(8,128)(2,1)} %copy-done.8) | copy-start | bytes 1572868
  132.0 4.8 %copy-start.12 = (bf16[24,16,1024]{2,1,0:T(8,128)(2,1)S(1)}, bf16[24,16,1024]{2,1,0:T(8,128)(2,1)}, u32[]{:S(2)}) copy-start(bf16[24,16,1024]{2,1,0:T(8,128)(2,1)} %copy-done.11) | copy-start | bytes 2359300
  132.0 4.8 %copy-start.15 = (bf16[16,16,1024]{2,1,0:T(8,128)(2,1)S(1)}, bf16[16,16,1024]{2,1,0:T(8,128)(2,1)}, u32[]{:S(2)}) copy-start(bf16[16,16,1024]{2,1,0:T(8,128)(2,1)} %copy-done.14) | copy-start | bytes 1572868
  132.0 4.8 %copy-start.19 = (bf16[16,16,1024]{2,1,0:T(8,128)(2,1)S(1)}, bf16[16,16,1024]{2,1,0:T(8,128)(2,1)}, u32[]{:S(2)}) copy-start(bf16[16,16,1024]{2,1,0:T(8,128)(2,1)} %copy-done.17) | copy-start | bytes 1572868
  132.0 4.8 %copy-start.23 = (bf16[16,16,1024]{2,1,0:T(8,128)(2,1)S(1)}, bf16[16,16,1024]{2,1,0:T(8,128)(2,1)}, u32[]{:S(2)}) copy-start(bf16[16,16,1024]{2,1,0:T(8,128)(2,1)} %copy-done.21) | copy-start | bytes 1572868
  132.0 4.8 %copy-start.27 = (bf16[16,16,1024]{2,1,0:T(8,128)(2,1)S(1)}, bf16[16,16,1024]{2,1,0:T(8,128)(2,1)}, u32[]{:S(2)}) copy-start(bf16[16,16,1024]{2,1,0:T(8,128)(2,1)} %copy-done.25) | copy-start | bytes 1572868
  132.0 4.8 %copy-start.31 = (bf16[16,16,1024]{2,1,0:T(8,128)(2,1)S(1)}, bf16[16,16,1024]{2,1,0:T(8,128)(2,1)}, u32[]{:S(2)}) copy-start(bf16[16,16,1024]{2,1,0:T(8,128)(2,1)} %copy-done.29) | copy-start | bytes 1572868
  132.1 4.8 %copy-start.34 = (bf16[24,16,1024]{2,1,0:T(8,128)(2,1)S(1)}, bf16[24,16,1024]{2,1,0:T(8,128)(2,1)}, u32[]{:S(2)}) copy-start(bf16[24,16,1024]{2,1,0:T(8,128)(2,1)} %copy-done.33) | copy-start | bytes 2359300
  132.1 4.8 %copy-start.39 = (bf16[16,16,1024]{2,1,0:T(8,128)(2,1)S(1)}, bf16[16,16,1024]{2,1,0:T(8,128)(2,1)}, u32[]{:S(2)}) copy-start(bf16[16,16,1024]{2,1,0:T(8,128)(2,1)} %copy-done.38) | copy-start | bytes 1572868
  132.1 4.8 %copy-start.42 = (bf16[16,16,1024]{2,1,0:T(8,128)(2,1)S(1)}, bf16[16,16,1024]{2,1,0:T(8,128)(2,1)}, u32[]{:S(2)}) copy-start(bf16[16,16,1024]{2,1,0:T(8,128)(2,1)} %copy-done.41) | copy-start | bytes 1572868
  132.1 4.8 %copy-start.45 = (bf16[16,16,1024]{2,1,0:T(8,128)(2,1)S(1)}, bf16[16,16,1024]{2,1,0:T(8,128)(2,1)}, u32[]{:S(2)}) copy-start(bf16[16,16,1024]{2,1,0:T(8,128)(2,1)} %copy-done.44) | copy-start | bytes 1572868
  132.1 4.8 %copy-start.48 = (bf16[16,16,1024]{2,1,0:T(8,128)(2,1)S(1)}, bf16[16,16,1024]{2,1,0:T(8,128)(2,1)}, u32[]{:S(2)}) copy-start(bf16[16,16,1024]{2,1,0:T(8,128)(2,1)} %copy-done.47) | copy-start | bytes 1572868
  132.1 9.9 %collective-permute-start.24 = (bf16[8,16,1024]{2,1,0:T(8,128)(2,1)S(1)}, bf16[8,16,1024]{2,1,0:T(8,128)(2,1)}, u32[]{:S(2)}, u32[]{:S(2)}) collective-permute-start(bf16[8,16,1024]{2,1,0:T(8,128)(2,1)S(1)} %get-tuple-element.167), channel_id=1, source_target_pairs={{0,2},{1,3},{2,0},{3,1},{4,6},{5,7},{6,4},{7,5},{8,10},{9,11},{10,... | collective-permute-start | bytes 786440 | tf_op jit(solution)/shard_map/ppermute | solution.py:684
  147.1 4.2 %collective-permute-start.29 = (bf16[64,16,1024]{2,1,0:T(8,128)(2,1)S(1)}, bf16[64,16,1024]{2,1,0:T(8,128)(2,1)S(1)}, u32[]{:S(2)}, u32[]{:S(2)}) collective-permute-start(bf16[64,16,1024]{2,1,0:T(8,128)(2,1)S(1)} %gather_give.5.refs_5_), channel_id=1, source_target_pairs={{0,1},{1,0},{2,3},{3,2},{4,5},{5,4},{6,7},{7,6},{8,9},{9,8},{10,11... | collective-permute-start | bytes 6291464 | tf_op jit(solution)/shard_map/ppermute | solution.py:701
  (9 other events, 26.0 us)
where the time goes:
time: 155 us; the launch traced here: 154 us
  starting transfers between devices  60.2 us (39%)
  Pallas kernels  55.4 us (36%)
  waiting for transfers between devices  34.4 us (22%)
  between operations  2.89 us (2%)
    ppermute x24, starting transfers between devices, ship(): lax.ppermute(part, 'pool', hops[port])  51.6 us
    ppermute x24, waiting for transfers between devices, ship(): lax.ppermute(part, 'pool', hops[port])  33.4 us
    pallas_call x9, Pallas kernels, pick(): pl.pallas_call(functools.partial(pick_kernel, time, [item[:2] for item in...  16 us
    pallas_call x4, Pallas kernels, attend(): pl.pallas_call(functools.partial(attend_kernel, head), grid_spec=pltpu.Pr...  14.1 us
    pallas_call x4, Pallas kernels, gather(): pl.pallas_call(functools.partial(gather_kernel, mode, low, [item[:2] for...  9.32 us
    pallas_call x1, Pallas kernels, decode_halves(): pl.pallas_call(halves_kernel, grid_spec=pltpu.PrefetchScalarGridSpec(num_...  7.73 us
    all_to_all x1, starting transfers between devices, local_lanes(): lax.all_to_all(partial, 'pool', split_axis=0, concat_axis=0, tiled=True)  7.65 us
    pallas_call x1, Pallas kernels, make_plan(): pl.pallas_call(plan_kernel, grid_spec=pltpu.PrefetchScalarGridSpec(num_sc...  4.29 us
  transfers between devices with their start and end apart: 27, of which 13 were waited for; matrix products, arithmetic and copies ran while one was open for 0% of the time, Pallas kernels for 27%

commit v1 on v0

--- a/solution.py
+++ b/solution.py
@@ -721,7 +721,8 @@
         if 1 <= time <= KVH:
             seen, _ = lax.optimization_barrier((plan, after))
             after = partial = attend(time - 1, seen, queries, anchors, by_token, lines, partial)
-    partial, _ = lax.optimization_barrier((partial, after))
+    arrived = next(item[2] for item in landed if item[:2] == (ROUNDS - 2, 0))
+    partial, _ = lax.optimization_barrier((partial, arrived))
     swapped = lax.all_to_all(partial, "pool", split_axis=0, concat_axis=0, tiled=True)
     attention = merge(plan, place, swapped, after)
     cache = finish_in_two(plan, place, own, landed, after, attention)

time: 155 us -> 169 us (1.090)
  starting transfers between devices: 60.2 us -> 71.5 us
    all_to_all x1, starting transfers between devices: 7.65 us -> 13.8 us  [local_lanes(): lax.all_to_all(partial, 'pool', split_axis=0, concat_axis=0, tiled=True)]
    ppermute x24, starting transfers between devices: 51.6 us -> 54.8 us  [ship(): lax.ppermute(part, 'pool', hops[port])]
    ppermute x24, waiting for transfers between devices: 33.4 us -> 35.8 us  [ship(): lax.ppermute(part, 'pool', hops[port])]
    ppermute x1, starting transfers between devices: 0.17 us -> 2.15 us  [finish_in_two(): other = lax.ppermute(give, 'pool', TWIN)]
  transfers between devices with their start and end apart: 27 -> 27, of which waited for: 13 -> 9; matrix products, arithmetic and copies ran while one was open for 0% -> 0% of each run, Pallas kernels for 27% -> 25%
where the time goes in v1:
time: 169 us; the launch traced here: 168 us
  starting transfers between devices  71.5 us (42%)
  Pallas kernels  56.7 us (34%)
  waiting for transfers between devices  35.9 us (21%)
  between operations  2.94 us (2%)
    ppermute x24, starting transfers between devices, ship(): lax.ppermute(part, 'pool', hops[port])  54.8 us
    ppermute x24, waiting for transfers between devices, ship(): lax.ppermute(part, 'pool', hops[port])  35.8 us
    pallas_call x9, Pallas kernels, pick(): pl.pallas_call(functools.partial(pick_kernel, time, [item[:2] for item in...  16.7 us
    pallas_call x4, Pallas kernels, attend(): pl.pallas_call(functools.partial(attend_kernel, head), grid_spec=pltpu.Pr...  14.1 us
    all_to_all x1, starting transfers between devices, local_lanes(): lax.all_to_all(partial, 'pool', split_axis=0, concat_axis=0, tiled=True)  13.8 us
    pallas_call x4, Pallas kernels, gather(): pl.pallas_call(functools.partial(gather_kernel, mode, low, [item[:2] for...  9.88 us
    pallas_call x1, Pallas kernels, decode_halves(): pl.pallas_call(halves_kernel, grid_spec=pltpu.PrefetchScalarGridSpec(num_...  7.71 us
    pallas_call x1, Pallas kernels, make_plan(): pl.pallas_call(plan_kernel, grid_spec=pltpu.PrefetchScalarGridSpec(num_sc...  4.29 us
  transfers between devices with their start and end apart: 27, of which 9 were waited for; matrix products, arithmetic and copies ran while one was open for 0% of the time, Pallas kernels for 25%

profile of v1, /device:TPU:11, one launch (start us, length us, event | category | flops | bytes accessed | tf_op | source)
XLA Modules:
  0.0 167.8 jit_solution(6232552308931945811)
XLA Ops:
  0.6 0.0 copy-start.53
  0.6 0.1 pad_add_fusion.place
  0.7 7.7 %decode_halves.1 = (bf16[64,16,1024]{2,1,0:T(8,128)(2,1)}, bf16[64,16,1024]{2,1,0:T(8,128)(2,1)S(1)}) custom-call(s32[2]{0:T(128)S(1)} %pad_add_fusion.place, s32[16,128]{1,0:T(8,128)} %bitcast.27, bf16[128,1024]{1,0:T(8,128)(2,1)} %val_anchor.7, bf16[15,128,1024]{2,1,0:T(8,128)(2,1)} %bitcast.12, f32[8,128]{1,0:T(8,128)} %bitcast.22), custom_call_target="tpu_custom_call" | custom-call | tf_op jit(solution)/shard_map/decode_halves/pallas_call | solution.py:475
  8.4 0.7 collective-permute-start.4
  9.2 4.3 %make_plan.1.plan.refs_2_.requests.after = s32[8,128]{1,0:T(8,128)S(1)} custom-call(s32[2]{0:T(128)S(1)} %pad_add_fusion.place, s32[16]{0:T(128)} %lengths.1, s32[16,128]{1,0:T(8,128)S(1)} %bitcast.28), custom_call_target="tpu_custom_call" | custom-call | tf_op jit(solution)/shard_map/make_plan/pallas_call | solution.py:401
  13.5 0.0 copy-start.1
  13.5 0.0 copy-start.38
  13.5 0.0 copy-start.52
  13.5 2.4 %pick_0.1 = (bf16[16,16,1024]{2,1,0:T(8,128)(2,1)S(1)}, bf16[16,16,1024]{2,1,0:T(8,128)(2,1)S(1)}, bf16[24,16,1024]{2,1,0:T(8,128)(2,1)S(1)}) custom-call(s32[8,128]{1,0:T(8,128)S(1)} %make_plan.1.plan.refs_2_.requests.after, s32[2]{0:T(128)S(1)} %pad_add_fusion.place, bf16[64,16,1024]{2,1,0:T(8,128)(2,1)} %get-tuple-element.141.refs_0_, ...), custom_call_target="tpu_custom_call" | custom-call | tf_op jit(solution)/shard_map/pick_0/pallas_call | solution.py:560
  15.9 3.2 %collective-permute-start.5 = (bf16[16,16,1024]{2,1,0:T(8,128)(2,1)S(1)}, bf16[16,16,1024]{2,1,0:T(8,128)(2,1)S(1)}, u32[]{:S(2)}, u32[]{:S(2)}) collective-permute-start(bf16[16,16,1024]{2,1,0:T(8,128)(2,1)S(1)} %get-tuple-element.143.refs_2_), channel_id=1, source_target_pairs={{0,4},{1,5},{2,6},{3,7},{4,8},{5,9},{6,10},{7,11},{8,12},{9,13},{1... | collective-permute-start | bytes 1572872 | tf_op jit(solution)/shard_map/ppermute | solution.py:684
  19.1 0.3 collective-permute-start.7
  19.4 2.1 %collective-permute-start.6 = (bf16[16,16,1024]{2,1,0:T(8,128)(2,1)S(1)}, bf16[16,16,1024]{2,1,0:T(8,128)(2,1)S(1)}, u32[]{:S(2)}, u32[]{:S(2)}) collective-permute-start(bf16[16,16,1024]{2,1,0:T(8,128)(2,1)S(1)} %get-tuple-element.144), channel_id=1, source_target_pairs={{4,0},{5,1},{6,2},{7,3},{8,4},{9,5},{10,6},{11,7},{12,8},{13,9},{1... | collective-permute-start | bytes 1572872 | tf_op jit(solution)/shard_map/ppermute | solution.py:684
  21.5 1.9 %pick_1.1 = (bf16[16,16,1024]{2,1,0:T(8,128)(2,1)S(1)}, bf16[16,16,1024]{2,1,0:T(8,128)(2,1)S(1)}) custom-call(s32[8,128]{1,0:T(8,128)S(1)} %make_plan.1.plan.refs_2_.requests.after, s32[2]{0:T(128)S(1)} %pad_add_fusion.place, bf16[64,16,1024]{2,1,0:T(8,128)(2,1)} %get-tuple-element.141.refs_0_, bf16[64,16,1024]{2,1,0:T(8,128)(2,1)} %collective-permute-done.4.refs_1_, ...), custom_call_target="tpu_custom_call" | custom-call | tf_op jit(solution)/shard_map/pick_1/pallas_call | solution.py:560
  23.4 3.1 %collective-permute-start.8 = (bf16[16,16,1024]{2,1,0:T(8,128)(2,1)S(1)}, bf16[16,16,1024]{2,1,0:T(8,128)(2,1)S(1)}, u32[]{:S(2)}, u32[]{:S(2)}) collective-permute-start(bf16[16,16,1024]{2,1,0:T(8,128)(2,1)S(1)} %get-tuple-element.146), channel_id=1, source_target_pairs={{0,4},{1,5},{2,6},{3,7},{4,8},{5,9},{6,10},{7,11},{8,12},{9,13},{1... | collective-permute-start | bytes 1572872 | tf_op jit(solution)/shard_map/ppermute | solution.py:684
  26.5 2.2 %collective-permute-start.9 = (bf16[16,16,1024]{2,1,0:T(8,128)(2,1)S(1)}, bf16[16,16,1024]{2,1,0:T(8,128)(2,1)S(1)}, u32[]{:S(2)}, u32[]{:S(2)}) collective-permute-start(bf16[16,16,1024]{2,1,0:T(8,128)(2,1)S(1)} %get-tuple-element.147), channel_id=1, source_target_pairs={{4,0},{5,1},{6,2},{7,3},{8,4},{9,5},{10,6},{11,7},{12,8},{13,9},{1... | collective-permute-start | bytes 1572872 | tf_op jit(solution)/shard_map/ppermute | solution.py:684
  28.8 3.4 %attend_0.1.refs_4_.after = bf16[16,112,128]{2,1,0:T(8,128)(2,1)} custom-call(s32[8,128]{1,0:T(8,128)S(1)} %make_plan.1.plan.refs_2_.requests.after, s32[8,128]{1,0:T(8,128)S(1)} %make_plan.1.plan.refs_2_.requests.after, bf16[16,8,8192]{2,1,0:T(8,128)(2,1)S(1)} %copy-done, bf16[16,8,8192]{2,1,0:T(8,128)(2,1)S(1)} %copy-done, ...), custom_call_target="tpu_custom_call" | custom-call | tf_op jit(solution)/shard_map/attend_0/pallas_call | solution.py:136
  32.2 2.1 %collective-permute-done.6.refs_3_ = bf16[16,16,1024]{2,1,0:T(8,128)(2,1)S(1)} collective-permute-done((bf16[16,16,1024]{2,1,0:T(8,128)(2,1)S(1)}, bf16[16,16,1024]{2,1,0:T(8,128)(2,1)S(1)}, u32[]{:S(2)}, u32[]{:S(2)}) %collective-permute-start.6) | collective-permute-done | bytes 524320 | tf_op jit(solution)/shard_map/ppermute | solution.py:684
  34.2 1.8 %pick_2.1 = (bf16[16,16,1024]{2,1,0:T(8,128)(2,1)S(1)}, bf16[16,16,1024]{2,1,0:T(8,128)(2,1)S(1)}, bf16[24,16,1024]{2,1,0:T(8,128)(2,1)S(1)}) custom-call(s32[8,128]{1,0:T(8,128)S(1)} %make_plan.1.plan.refs_2_.requests.after, s32[2]{0:T(128)S(1)} %pad_add_fusion.place, bf16[64,16,1024]{2,1,0:T(8,128)(2,1)} %get-tuple-element.141.refs_0_, ...), custom_call_target="tpu_custom_call" | custom-call | tf_op jit(solution)/shard_map/pick_2/pallas_call | solution.py:560
  36.0 3.0 %collective-permute-start.10 = (bf16[16,16,1024]{2,1,0:T(8,128)(2,1)S(1)}, bf16[16,16,1024]{2,1,0:T(8,128)(2,1)S(1)}, u32[]{:S(2)}, u32[]{:S(2)}) collective-permute-start(bf16[16,16,1024]{2,1,0:T(8,128)(2,1)S(1)} %get-tuple-element.149), channel_id=1, source_target_pairs={{0,4},{1,5},{2,6},{3,7},{4,8},{5,9},{6,10},{7,11},{8,12},{9,13},{1... | collective-permute-start | bytes 1572872 | tf_op jit(solution)/shard_map/ppermute | solution.py:684
  39.0 1.4 collective-permute-start.12
  40.4 2.2 %collective-permute-done.8.refs_5_ = bf16[16,16,1024]{2,1,0:T(8,128)(2,1)S(1)} collective-permute-done((bf16[16,16,1024]{2,1,0:T(8,128)(2,1)S(1)}, bf16[16,16,1024]{2,1,0:T(8,128)(2,1)S(1)}, u32[]{:S(2)}, u32[]{:S(2)}) %collective-permute-start.8) | collective-permute-done | bytes 524320 | tf_op jit(solution)/shard_map/ppermute | solution.py:684
  42.6 1.9 %collective-permute-start.11 = (bf16[16,16,1024]{2,1,0:T(8,128)(2,1)S(1)}, bf16[16,16,1024]{2,1,0:T(8,128)(2,1)S(1)}, u32[]{:S(2)}, u32[]{:S(2)}) collective-permute-start(bf16[16,16,1024]{2,1,0:T(8,128)(2,1)S(1)} %get-tuple-element.150), channel_id=1, source_target_pairs={{4,0},{5,1},{6,2},{7,3},{8,4},{9,5},{10,6},{11,7},{12,8},{13,9},{1... | collective-permute-start | bytes 1572872 | tf_op jit(solution)/shard_map/ppermute | solution.py:684
  44.5 3.4 %attend_1.1.refs_7_.after = bf16[16,112,128]{2,1,0:T(8,128)(2,1)} custom-call(s32[8,128]{1,0:T(8,128)S(1)} %make_plan.1.plan.refs_2_.requests.after, s32[8,128]{1,0:T(8,128)S(1)} %make_plan.1.plan.refs_2_.requests.after, bf16[16,8,8192]{2,1,0:T(8,128)(2,1)S(1)} %copy-done, bf16[16,8,8192]{2,1,0:T(8,128)(2,1)S(1)} %copy-done, ...), custom_call_target="tpu_custom_call", output_to_operand_aliasing={{}: (10, {})} | custom-call | tf_op jit(solution)/shard_map/attend_1/pallas_call | solution.py:136
  47.9 1.7 %pick_3.1 = (bf16[16,16,1024]{2,1,0:T(8,128)(2,1)S(1)}, bf16[16,16,1024]{2,1,0:T(8,128)(2,1)S(1)}) custom-call(s32[8,128]{1,0:T(8,128)S(1)} %make_plan.1.plan.refs_2_.requests.after, s32[2]{0:T(128)S(1)} %pad_add_fusion.place, bf16[64,16,1024]{2,1,0:T(8,128)(2,1)} %get-tuple-element.141.refs_0_, bf16[64,16,1024]{2,1,0:T(8,128)(2,1)} %collective-permute-done.4.refs_1_, ...), custom_call_target="tpu_custom_call" | custom-call | tf_op jit(solution)/shard_map/pick_3/pallas_call | solution.py:560
  49.6 2.5 %collective-permute-start.13 = (bf16[16,16,1024]{2,1,0:T(8,128)(2,1)S(1)}, bf16[16,16,1024]{2,1,0:T(8,128)(2,1)S(1)}, u32[]{:S(2)}, u32[]{:S(2)}) collective-permute-start(bf16[16,16,1024]{2,1,0:T(8,128)(2,1)S(1)} %get-tuple-element.153), channel_id=1, source_target_pairs={{0,4},{1,5},{2,6},{3,7},{4,8},{5,9},{6,10},{7,11},{8,12},{9,13},{1... | collective-permute-start | bytes 1572872 | tf_op jit(solution)/shard_map/ppermute | solution.py:684
  52.1 2.8 %collective-permute-start.14 = (bf16[16,16,1024]{2,1,0:T(8,128)(2,1)S(1)}, bf16[16,16,1024]{2,1,0:T(8,128)(2,1)}, u32[]{:S(2)}, u32[]{:S(2)}) collective-permute-start(bf16[16,16,1024]{2,1,0:T(8,128)(2,1)S(1)} %get-tuple-element.154), channel_id=1, source_target_pairs={{4,0},{5,1},{6,2},{7,3},{8,4},{9,5},{10,6},{11,7},{12,8},{13,9},{1... | collective-permute-start | bytes 1572872 | tf_op jit(solution)/shard_map/ppermute | solution.py:684
  54.9 3.4 %attend_2.1.refs_9_.after = bf16[16,112,128]{2,1,0:T(8,128)(2,1)} custom-call(s32[8,128]{1,0:T(8,128)S(1)} %make_plan.1.plan.refs_2_.requests.after, s32[8,128]{1,0:T(8,128)S(1)} %make_plan.1.plan.refs_2_.requests.after, bf16[16,8,8192]{2,1,0:T(8,128)(2,1)S(1)} %copy-done, bf16[16,8,8192]{2,1,0:T(8,128)(2,1)S(1)} %copy-done, ...), custom_call_target="tpu_custom_call", output_to_operand_aliasing={{}: (10, {})} | custom-call | tf_op jit(solution)/shard_map/attend_2/pallas_call | solution.py:136
  58.3 1.0 pick_4.1
  59.4 0.1 collective-permute-start.17
  59.5 3.7 %collective-permute-start.15 = (bf16[16,16,1024]{2,1,0:T(8,128)(2,1)S(1)}, bf16[16,16,1024]{2,1,0:T(8,128)(2,1)S(1)}, u32[]{:S(2)}, u32[]{:S(2)}) collective-permute-start(bf16[16,16,1024]{2,1,0:T(8,128)(2,1)S(1)} %get-tuple-element.156), channel_id=1, source_target_pairs={{0,4},{1,5},{2,6},{3,7},{4,8},{5,9},{6,10},{7,11},{8,12},{9,13},{1... | collective-permute-start | bytes 1572872 | tf_op jit(solution)/shard_map/ppermute | solution.py:684
  63.1 4.0 %attend_3.1.refs_12_ = bf16[16,112,128]{2,1,0:T(8,128)(2,1)} custom-call(s32[8,128]{1,0:T(8,128)S(1)} %make_plan.1.plan.refs_2_.requests.after, s32[8,128]{1,0:T(8,128)S(1)} %make_plan.1.plan.refs_2_.requests.after, bf16[16,8,8192]{2,1,0:T(8,128)(2,1)S(1)} %copy-done, bf16[16,8,8192]{2,1,0:T(8,128)(2,1)S(1)} %copy-done, ...), custom_call_target="tpu_custom_call", output_to_operand_aliasing={{}: (10, {})} | custom-call | tf_op jit(solution)/shard_map/attend_3/pallas_call | solution.py:136
  67.2 1.9 %collective-permute-start.16 = (bf16[16,16,1024]{2,1,0:T(8,128)(2,1)S(1)}, bf16[16,16,1024]{2,1,0:T(8,128)(2,1)S(1)}, u32[]{:S(2)}, u32[]{:S(2)}) collective-permute-start(bf16[16,16,1024]{2,1,0:T(8,128)(2,1)S(1)} %get-tuple-element.157), channel_id=1, source_target_pairs={{4,0},{5,1},{6,2},{7,3},{8,4},{9,5},{10,6},{11,7},{12,8},{13,9},{1... | collective-permute-start | bytes 1572872 | tf_op jit(solution)/shard_map/ppermute | solution.py:684
  69.1 1.9 %pick_5.1 = (bf16[16,16,1024]{2,1,0:T(8,128)(2,1)S(1)}, bf16[16,16,1024]{2,1,0:T(8,128)(2,1)S(1)}) custom-call(s32[8,128]{1,0:T(8,128)S(1)} %make_plan.1.plan.refs_2_.requests.after, s32[2]{0:T(128)S(1)} %pad_add_fusion.place, bf16[64,16,1024]{2,1,0:T(8,128)(2,1)} %get-tuple-element.141.refs_0_, bf16[64,16,1024]{2,1,0:T(8,128)(2,1)} %collective-permute-done.4.refs_1_, ...), custom_call_target="tpu_custom_call" | custom-call | tf_op jit(solution)/shard_map/pick_5/pallas_call | solution.py:560
  71.0 3.8 %collective-permute-start.18 = (bf16[16,16,1024]{2,1,0:T(8,128)(2,1)S(1)}, bf16[16,16,1024]{2,1,0:T(8,128)(2,1)S(1)}, u32[]{:S(2)}, u32[]{:S(2)}) collective-permute-start(bf16[16,16,1024]{2,1,0:T(8,128)(2,1)S(1)} %get-tuple-element.160.refs_14_), channel_id=1, source_target_pairs={{0,4},{1,5},{2,6},{3,7},{4,8},{5,9},{6,10},{7,11},{8,12},{9,13},{1... | collective-permute-start | bytes 1572872 | tf_op jit(solution)/shard_map/ppermute | solution.py:684
  74.9 2.1 %collective-permute-start.19 = (bf16[16,16,1024]{2,1,0:T(8,128)(2,1)S(1)}, bf16[16,16,1024]{2,1,0:T(8,128)(2,1)S(1)}, u32[]{:S(2)}, u32[]{:S(2)}) collective-permute-start(bf16[16,16,1024]{2,1,0:T(8,128)(2,1)S(1)} %get-tuple-element.161), channel_id=1, source_target_pairs={{4,0},{5,1},{6,2},{7,3},{8,4},{9,5},{10,6},{11,7},{12,8},{13,9},{1... | collective-permute-start | bytes 1572872 | tf_op jit(solution)/shard_map/ppermute | solution.py:684
  77.0 4.6 %collective-permute-done.16.refs_13_ = bf16[16,16,1024]{2,1,0:T(8,128)(2,1)S(1)} collective-permute-done((bf16[16,16,1024]{2,1,0:T(8,128)(2,1)S(1)}, bf16[16,16,1024]{2,1,0:T(8,128)(2,1)S(1)}, u32[]{:S(2)}, u32[]{:S(2)}) %collective-permute-start.16) | collective-permute-done | bytes 524320 | tf_op jit(solution)/shard_map/ppermute | solution.py:684
  81.6 1.7 %pick_6.1 = (bf16[16,16,1024]{2,1,0:T(8,128)(2,1)S(1)}, bf16[16,16,1024]{2,1,0:T(8,128)(2,1)S(1)}, bf16[16,16,1024]{2,1,0:T(8,128)(2,1)S(1)}) custom-call(s32[8,128]{1,0:T(8,128)S(1)} %make_plan.1.plan.refs_2_.requests.after, s32[2]{0:T(128)S(1)} %pad_add_fusion.place, bf16[64,16,1024]{2,1,0:T(8,128)(2,1)} %get-tuple-element.141.refs_0_, ...), custom_call_target="tpu_custom_call" | custom-call | tf_op jit(solution)/shard_map/pick_6/pallas_call | solution.py:560
  83.3 2.3 %collective-permute-done.18.refs_15_ = bf16[16,16,1024]{2,1,0:T(8,128)(2,1)S(1)} collective-permute-done((bf16[16,16,1024]{2,1,0:T(8,128)(2,1)S(1)}, bf16[16,16,1024]{2,1,0:T(8,128)(2,1)S(1)}, u32[]{:S(2)}, u32[]{:S(2)}) %collective-permute-start.18) | collective-permute-done | bytes 524320 | tf_op jit(solution)/shard_map/ppermute | solution.py:684
  85.6 7.2 %collective-permute-done.19.refs_16_ = bf16[16,16,1024]{2,1,0:T(8,128)(2,1)S(1)} collective-permute-done((bf16[16,16,1024]{2,1,0:T(8,128)(2,1)S(1)}, bf16[16,16,1024]{2,1,0:T(8,128)(2,1)S(1)}, u32[]{:S(2)}, u32[]{:S(2)}) %collective-permute-start.19) | collective-permute-done | bytes 524320 | tf_op jit(solution)/shard_map/ppermute | solution.py:684
  92.9 1.9 %pick_7.1 = (bf16[16,16,1024]{2,1,0:T(8,128)(2,1)S(1)}, bf16[16,16,1024]{2,1,0:T(8,128)(2,1)}, bf16[16,16,1024]{2,1,0:T(8,128)(2,1)S(1)}) custom-call(s32[8,128]{1,0:T(8,128)S(1)} %make_plan.1.plan.refs_2_.requests.after, s32[2]{0:T(128)S(1)} %pad_add_fusion.place, bf16[64,16,1024]{2,1,0:T(8,128)(2,1)} %get-tuple-element.141.refs_0_, ...), custom_call_target="tpu_custom_call" | custom-call | tf_op jit(solution)/shard_map/pick_7/pallas_call | solution.py:560
  94.8 3.8 %collective-permute-start.26 = (bf16[16,16,1024]{2,1,0:T(8,128)(2,1)S(1)}, bf16[16,16,1024]{2,1,0:T(8,128)(2,1)}, u32[]{:S(2)}, u32[]{:S(2)}) collective-permute-start(bf16[16,16,1024]{2,1,0:T(8,128)(2,1)S(1)} %get-tuple-element.164.refs_19_), channel_id=1, source_target_pairs={{0,4},{1,5},{2,6},{3,7},{4,8},{5,9},{6,10},{7,11},{8,12},{9,13},{1... | collective-permute-start | bytes 1572872 | tf_op jit(solution)/shard_map/ppermute | solution.py:684
  98.6 1.9 %collective-permute-start.20 = (bf16[16,16,1024]{2,1,0:T(8,128)(2,1)S(1)}, bf16[16,16,1024]{2,1,0:T(8,128)(2,1)}, u32[]{:S(2)}, u32[]{:S(2)}) collective-permute-start(bf16[16,16,1024]{2,1,0:T(8,128)(2,1)S(1)} %get-tuple-element.162.refs_17_), channel_id=1, source_target_pairs={{0,4},{1,5},{2,6},{3,7},{4,8},{5,9},{6,10},{7,11},{8,12},{9,13},{1... | collective-permute-start | bytes 1572872 | tf_op jit(solution)/shard_map/ppermute | solution.py:684
  100.5 4.1 %collective-permute-start.21 = (bf16[16,16,1024]{2,1,0:T(8,128)(2,1)S(1)}, bf16[16,16,1024]{2,1,0:T(8,128)(2,1)}, u32[]{:S(2)}, u32[]{:S(2)}) collective-permute-start(bf16[16,16,1024]{2,1,0:T(8,128)(2,1)S(1)} %get-tuple-element.163), channel_id=1, source_target_pairs={{4,0},{5,1},{6,2},{7,3},{8,4},{9,5},{10,6},{11,7},{12,8},{13,9},{1... | collective-permute-start | bytes 1572872 | tf_op jit(solution)/shard_map/ppermute | solution.py:684
  104.7 2.3 %collective-permute-done.26.refs_20_ = bf16[16,16,1024]{2,1,0:T(8,128)(2,1)} collective-permute-done((bf16[16,16,1024]{2,1,0:T(8,128)(2,1)S(1)}, bf16[16,16,1024]{2,1,0:T(8,128)(2,1)}, u32[]{:S(2)}, u32[]{:S(2)}) %collective-permute-start.26) | collective-permute-done | bytes 524320 | tf_op jit(solution)/shard_map/ppermute | solution.py:684
  107.0 13.8 %all-to-all-start.1 = ((bf16[16,112,128]{2,1,0:T(8,128)(2,1)}), bf16[16,112,128]{2,1,0:T(8,128)(2,1)S(1)}, u32[]{:S(2)}, u32[]{:S(2)}) async-start(bf16[16,112,128]{2,1,0:T(8,128)(2,1)} %attend_3.1.refs_12_), calls=%async_computation.1 | async-start | bytes 917504 | tf_op jit(solution)/shard_map/all_to_all | solution.py:726
  120.8 0.3 collective-permute-start.25
  121.0 2.0 %collective-permute-start.27 = (bf16[16,16,1024]{2,1,0:T(8,128)(2,1)}, bf16[16,16,1024]{2,1,0:T(8,128)(2,1)S(1)}, u32[]{:S(2)}, u32[]{:S(2)}) collective-permute-start(bf16[16,16,1024]{2,1,0:T(8,128)(2,1)} %get-tuple-element.169), channel_id=1, source_target_pairs={{4,0},{5,1},{6,2},{7,3},{8,4},{9,5},{10,6},{11,7},{12,8},{13,9},{1... | collective-permute-start | bytes 1572872 | tf_op jit(solution)/shard_map/ppermute | solution.py:684
  123.1 1.5 collective-permute-start.28
  124.6 2.5 %pick_8.1 = (bf16[16,16,1024]{2,1,0:T(8,128)(2,1)S(1)}, bf16[16,16,1024]{2,1,0:T(8,128)(2,1)}, bf16[8,16,1024]{2,1,0:T(8,128)(2,1)S(1)}) custom-call(s32[8,128]{1,0:T(8,128)S(1)} %make_plan.1.plan.refs_2_.requests.after, s32[2]{0:T(128)S(1)} %pad_add_fusion.place, bf16[64,16,1024]{2,1,0:T(8,128)(2,1)} %get-tuple-element.141.refs_0_, ...), custom_call_target="tpu_custom_call" | custom-call | tf_op jit(solution)/shard_map/pick_8/pallas_call | solution.py:560
  127.1 3.3 %collective-permute-start.22 = (bf16[16,16,1024]{2,1,0:T(8,128)(2,1)S(1)}, bf16[16,16,1024]{2,1,0:T(8,128)(2,1)}, u32[]{:S(2)}, u32[]{:S(2)}) collective-permute-start(bf16[16,16,1024]{2,1,0:T(8,128)(2,1)S(1)} %get-tuple-element.165.refs_23_.after), channel_id=1, source_target_pairs={{0,4},{1,5},{2,6},{3,7},{4,8},{5,9},{6,10},{7,11},{8,12},{9,13},{1... | collective-permute-start | bytes 1572872 | tf_op jit(solution)/shard_map/ppermute | solution.py:684
  130.4 2.8 %collective-permute-start.23 = (bf16[16,16,1024]{2,1,0:T(8,128)(2,1)}, bf16[16,16,1024]{2,1,0:T(8,128)(2,1)}, u32[]{:S(2)}, u32[]{:S(2)}) collective-permute-start(bf16[16,16,1024]{2,1,0:T(8,128)(2,1)} %get-tuple-element.166), channel_id=1, source_target_pairs={{4,0},{5,1},{6,2},{7,3},{8,4},{9,5},{10,6},{11,7},{12,8},{13,9},{1... | collective-permute-start | bytes 1572872 | tf_op jit(solution)/shard_map/ppermute | solution.py:684
  133.2 5.1 %collective-permute-done.25.refs_19_ = bf16[16,16,1024]{2,1,0:T(8,128)(2,1)S(1)} collective-permute-done((bf16[16,16,1024]{2,1,0:T(8,128)(2,1)S(1)}, bf16[16,16,1024]{2,1,0:T(8,128)(2,1)S(1)}, u32[]{:S(2)}, u32[]{:S(2)}) %collective-permute-start.25) | collective-permute-done | bytes 524320 | tf_op jit(solution)/shard_map/ppermute | solution.py:684
  138.3 1.1 collective-permute-start.24
  139.4 4.5 %collective-permute-done.27.refs_21_ = bf16[16,16,1024]{2,1,0:T(8,128)(2,1)S(1)} collective-permute-done((bf16[16,16,1024]{2,1,0:T(8,128)(2,1)}, bf16[16,16,1024]{2,1,0:T(8,128)(2,1)S(1)}, u32[]{:S(2)}, u32[]{:S(2)}) %collective-permute-start.27) | collective-permute-done | bytes 524320 | tf_op jit(solution)/shard_map/ppermute | solution.py:684
  144.0 5.6 %collective-permute-done.28.refs_22_ = bf16[16,16,1024]{2,1,0:T(8,128)(2,1)S(1)} collective-permute-done((bf16[16,16,1024]{2,1,0:T(8,128)(2,1)S(1)}, bf16[16,16,1024]{2,1,0:T(8,128)(2,1)S(1)}, u32[]{:S(2)}, u32[]{:S(2)}) %collective-permute-start.28) | collective-permute-done | bytes 524320 | tf_op jit(solution)/shard_map/ppermute | solution.py:684
  149.7 2.8 %gather_give.4.refs_6_ = bf16[64,16,1024]{2,1,0:T(8,128)(2,1)S(1)} custom-call(s32[8,128]{1,0:T(8,128)S(1)} %make_plan.1.plan.refs_2_.requests.after, s32[2]{0:T(128)S(1)} %pad_add_fusion.place, bf16[64,16,1024]{2,1,0:T(8,128)(2,1)} %get-tuple-element.141.refs_0_, bf16[64,16,1024]{2,1,0:T(8,128)(2,1)} %collective-permute-done.4.refs_1_, ...), custom_call_target="tpu_custom_call" | custom-call | tf_op jit(solution)/shard_map/gather_give/pallas_call | solution.py:614
  152.5 3.2 %gather_own.4.refs_5_.refs_6_ = bf16[128,16,1024]{2,1,0:T(8,128)(2,1)} custom-call(s32[8,128]{1,0:T(8,128)S(1)} %make_plan.1.plan.refs_2_.requests.after, s32[2]{0:T(128)S(1)} %pad_add_fusion.place, bf16[64,16,1024]{2,1,0:T(8,128)(2,1)} %get-tuple-element.141.refs_0_, bf16[64,16,1024]{2,1,0:T(8,128)(2,1)} %collective-permute-done.4.refs_1_, ...), custom_call_target="tpu_custom_call" | custom-call | tf_op jit(solution)/shard_map/gather_own/pallas_call | solution.py:614
  155.7 1.8 %merge.1 = bf16[16,8,512]{2,1,0:T(8,128)(2,1)} custom-call(s32[8,128]{1,0:T(8,128)S(1)} %make_plan.1.plan.refs_2_.requests.after, s32[2]{0:T(128)S(1)} %pad_add_fusion.place, bf16[16,112,128]{2,1,0:T(8,128)(2,1)S(1)} %all-to-all-done.1.parts, bf16[16,16,1024]{2,1,0:T(8,128)(2,1)S(1)} %get-tuple-element.165.refs_23_.after), custom_call_target="tpu_custom_call" | custom-call | tf_op jit(solution)/shard_map/merge/pallas_call | solution.py:202
  157.5 1.2 gather_give.5.refs_5_
  158.8 2.2 %collective-permute-start.29 = (bf16[64,16,1024]{2,1,0:T(8,128)(2,1)S(1)}, bf16[64,16,1024]{2,1,0:T(8,128)(2,1)S(1)}, u32[]{:S(2)}, u32[]{:S(2)}) collective-permute-start(bf16[64,16,1024]{2,1,0:T(8,128)(2,1)S(1)} %gather_give.5.refs_5_), channel_id=1, source_target_pairs={{0,1},{1,0},{2,3},{3,2},{4,5},{5,4},{6,7},{7,6},{8,9},{9,8},{10,11... | collective-permute-start | bytes 6291464 | tf_op jit(solution)/shard_map/ppermute | solution.py:701
  160.9 0.5 slice.3
  162.8 2.7 %gather_own.5.cache = bf16[128,16,1024]{2,1,0:T(8,128)(2,1)} custom-call(s32[8,128]{1,0:T(8,128)S(1)} %make_plan.1.plan.refs_2_.requests.after, s32[2]{0:T(128)S(1)} %pad_add_fusion.place, bf16[64,16,1024]{2,1,0:T(8,128)(2,1)} %get-tuple-element.141.refs_0_, bf16[64,16,1024]{2,1,0:T(8,128)(2,1)} %collective-permute-done.4.refs_1_, ...), custom_call_target="tpu_custom_call", output_to_operand_aliasing={{}: (8, {})} | custom-call | tf_op jit(solution)/shard_map/gather_own/pallas_call | solution.py:614
  165.5 2.1 %fill.3 = bf16[128,16,1024]{2,1,0:T(8,128)(2,1)} custom-call(s32[2]{0:T(128)S(1)} %pad_add_fusion.place, bf16[128,16,1024]{2,1,0:T(8,128)(2,1)} %gather_own.5.cache, bf16[64,16,1024]{2,1,0:T(8,128)(2,1)S(1)} %collective-permute-done.29.other), custom_call_target="tpu_custom_call", output_to_operand_aliasing={{}: (1, {})} | custom-call | tf_op jit(solution)/shard_map/fill/pallas_call | solution.py:655
  167.7 0.0 copy-done.16
  (100 shorter events, 0.2 us)
Async XLA Ops:
  0.6 8.6 %copy-start.53 = (s32[2048]{0:T(1024)S(1)}, s32[2048]{0:T(1024)}, u32[]{:S(2)}) copy-start(s32[2048]{0:T(1024)} %param.14) | copy-start | bytes 24580
  8.4 5.0 %collective-permute-start.4 = (bf16[64,16,1024]{2,1,0:T(8,128)(2,1)S(1)}, bf16[64,16,1024]{2,1,0:T(8,128)(2,1)}, u32[]{:S(2)}, u32[]{:S(2)}) collective-permute-start(bf16[64,16,1024]{2,1,0:T(8,128)(2,1)S(1)} %get-tuple-element.142), channel_id=1, source_target_pairs={{0,1},{1,0},{2,3},{3,2},{4,5},{5,4},{6,7},{7,6},{8,9},{9,8},{10,11... | collective-permute-start | bytes 6291464 | tf_op jit(solution)/shard_map/ppermute | solution.py:712
  13.5 15.3 %copy-start = (bf16[16,8,8192]{2,1,0:T(8,128)(2,1)S(1)}, bf16[16,8,8192]{2,1,0:T(8,128)(2,1)}, u32[]{:S(2)}) copy-start(bf16[16,8,8192]{2,1,0:T(8,128)(2,1)} %third.7) | copy-start | bytes 6291460
  13.5 15.3 %copy-start.1 = (bf16[128,15,1024]{2,0,1:T(8,128)(2,1)S(1)}, bf16[128,15,1024]{2,0,1:T(8,128)(2,1)}, u32[]{:S(2)}) copy-start(bf16[128,15,1024]{2,0,1:T(8,128)(2,1)} %param.10) | copy-start | bytes 11796484
  13.5 15.3 %copy-start.38 = (bf16[128,1024]{1,0:T(8,128)(2,1)S(1)}, bf16[128,1024]{1,0:T(8,128)(2,1)}, u32[]{:S(2)}) copy-start(bf16[128,1024]{1,0:T(8,128)(2,1)} %val_anchor.7) | copy-start | bytes 786436
  13.5 15.3 %copy-start.52 = (f32[128,8]{0,1:T(8,128)S(1)}, f32[128,8]{0,1:T(8,128)}, u32[]{:S(2)}) copy-start(f32[128,8]{0,1:T(8,128)} %param.11) | copy-start | bytes 12292
  15.9 16.2 %collective-permute-start.5 = (bf16[16,16,1024]{2,1,0:T(8,128)(2,1)S(1)}, bf16[16,16,1024]{2,1,0:T(8,128)(2,1)S(1)}, u32[]{:S(2)}, u32[]{:S(2)}) collective-permute-start(bf16[16,16,1024]{2,1,0:T(8,128)(2,1)S(1)} %get-tuple-element.143.refs_2_), channel_id=1, source_target_pairs={{0,4},{1,5},{2,6},{3,7},{4,8},{5,9},{6,10},{7,11},{8,12},{9,13},{1... | collective-permute-start | bytes 1572872 | tf_op jit(solution)/shard_map/ppermute | solution.py:684
  19.1 28.7 %collective-permute-start.7 = (bf16[24,16,1024]{2,1,0:T(8,128)(2,1)S(1)}, bf16[24,16,1024]{2,1,0:T(8,128)(2,1)S(1)}, u32[]{:S(2)}, u32[]{:S(2)}) collective-permute-start(bf16[24,16,1024]{2,1,0:T(8,128)(2,1)S(1)} %get-tuple-element.145), channel_id=1, source_target_pairs={{0,2},{1,3},{2,0},{3,1},{4,6},{5,7},{6,4},{7,5},{8,10},{9,11},{10,... | collective-permute-start | bytes 2359304 | tf_op jit(solution)/shard_map/ppermute | solution.py:684
  19.4 14.8 %collective-permute-start.6 = (bf16[16,16,1024]{2,1,0:T(8,128)(2,1)S(1)}, bf16[16,16,1024]{2,1,0:T(8,128)(2,1)S(1)}, u32[]{:S(2)}, u32[]{:S(2)}) collective-permute-start(bf16[16,16,1024]{2,1,0:T(8,128)(2,1)S(1)} %get-tuple-element.144), channel_id=1, source_target_pairs={{4,0},{5,1},{6,2},{7,3},{8,4},{9,5},{10,6},{11,7},{12,8},{13,9},{1... | collective-permute-start | bytes 1572872 | tf_op jit(solution)/shard_map/ppermute | solution.py:684
  23.4 19.2 %collective-permute-start.8 = (bf16[16,16,1024]{2,1,0:T(8,128)(2,1)S(1)}, bf16[16,16,1024]{2,1,0:T(8,128)(2,1)S(1)}, u32[]{:S(2)}, u32[]{:S(2)}) collective-permute-start(bf16[16,16,1024]{2,1,0:T(8,128)(2,1)S(1)} %get-tuple-element.146), channel_id=1, source_target_pairs={{0,4},{1,5},{2,6},{3,7},{4,8},{5,9},{6,10},{7,11},{8,12},{9,13},{1... | collective-permute-start | bytes 1572872 | tf_op jit(solution)/shard_map/ppermute | solution.py:684
  26.5 21.3 %collective-permute-start.9 = (bf16[16,16,1024]{2,1,0:T(8,128)(2,1)S(1)}, bf16[16,16,1024]{2,1,0:T(8,128)(2,1)S(1)}, u32[]{:S(2)}, u32[]{:S(2)}) collective-permute-start(bf16[16,16,1024]{2,1,0:T(8,128)(2,1)S(1)} %get-tuple-element.147), channel_id=1, source_target_pairs={{4,0},{5,1},{6,2},{7,3},{8,4},{9,5},{10,6},{11,7},{12,8},{13,9},{1... | collective-permute-start | bytes 1572872 | tf_op jit(solution)/shard_map/ppermute | solution.py:684
  32.2 60.7 %copy-start.5 = (bf16[16,16,1024]{2,1,0:T(8,128)(2,1)}, bf16[16,16,1024]{2,1,0:T(8,128)(2,1)S(1)}, u32[]{:S(2)}) copy-start(bf16[16,16,1024]{2,1,0:T(8,128)(2,1)S(1)} %collective-permute-done.5.refs_2_) | copy-start | bytes 1572868
  34.2 58.6 %copy-start.8 = (bf16[16,16,1024]{2,1,0:T(8,128)(2,1)}, bf16[16,16,1024]{2,1,0:T(8,128)(2,1)S(1)}, u32[]{:S(2)}) copy-start(bf16[16,16,1024]{2,1,0:T(8,128)(2,1)S(1)} %collective-permute-done.6.refs_3_) | copy-start | bytes 1572868
  36.0 22.3 %collective-permute-start.10 = (bf16[16,16,1024]{2,1,0:T(8,128)(2,1)S(1)}, bf16[16,16,1024]{2,1,0:T(8,128)(2,1)S(1)}, u32[]{:S(2)}, u32[]{:S(2)}) collective-permute-start(bf16[16,16,1024]{2,1,0:T(8,128)(2,1)S(1)} %get-tuple-element.149), channel_id=1, source_target_pairs={{0,4},{1,5},{2,6},{3,7},{4,8},{5,9},{6,10},{7,11},{8,12},{9,13},{1... | collective-permute-start | bytes 1572872 | tf_op jit(solution)/shard_map/ppermute | solution.py:684
  39.0 30.1 %collective-permute-start.12 = (bf16[24,16,1024]{2,1,0:T(8,128)(2,1)S(1)}, bf16[24,16,1024]{2,1,0:T(8,128)(2,1)S(1)}, u32[]{:S(2)}, u32[]{:S(2)}) collective-permute-start(bf16[24,16,1024]{2,1,0:T(8,128)(2,1)S(1)} %get-tuple-element.151), channel_id=1, source_target_pairs={{0,2},{1,3},{2,0},{3,1},{4,6},{5,7},{6,4},{7,5},{8,10},{9,11},{10,... | collective-permute-start | bytes 2359304 | tf_op jit(solution)/shard_map/ppermute | solution.py:684
  42.6 39.0 %copy-start.14 = (bf16[16,16,1024]{2,1,0:T(8,128)(2,1)}, bf16[16,16,1024]{2,1,0:T(8,128)(2,1)S(1)}, u32[]{:S(2)}) copy-start(bf16[16,16,1024]{2,1,0:T(8,128)(2,1)S(1)} %collective-permute-done.8.refs_5_) | copy-start | bytes 1572868
  42.6 15.7 %collective-permute-start.11 = (bf16[16,16,1024]{2,1,0:T(8,128)(2,1)S(1)}, bf16[16,16,1024]{2,1,0:T(8,128)(2,1)S(1)}, u32[]{:S(2)}, u32[]{:S(2)}) collective-permute-start(bf16[16,16,1024]{2,1,0:T(8,128)(2,1)S(1)} %get-tuple-element.150), channel_id=1, source_target_pairs={{4,0},{5,1},{6,2},{7,3},{8,4},{9,5},{10,6},{11,7},{12,8},{13,9},{1... | collective-permute-start | bytes 1572872 | tf_op jit(solution)/shard_map/ppermute | solution.py:684
  47.9 7.1 %copy-start.39 = (bf16[128,1024]{1,0:T(8,128)(2,1)S(1)}, bf16[128,1024]{1,0:T(8,128)(2,1)}, u32[]{:S(2)}) copy-start(bf16[128,1024]{1,0:T(8,128)(2,1)} %val_anchor.7) | copy-start | bytes 786436
  47.9 33.7 %copy-start.17 = (bf16[16,16,1024]{2,1,0:T(8,128)(2,1)}, bf16[16,16,1024]{2,1,0:T(8,128)(2,1)S(1)}, u32[]{:S(2)}) copy-start(bf16[16,16,1024]{2,1,0:T(8,128)(2,1)S(1)} %collective-permute-done.9.refs_6_) | copy-start | bytes 1572868
  47.9 45.0 %copy-start.2 = (bf16[24,16,1024]{2,1,0:T(8,128)(2,1)}, bf16[24,16,1024]{2,1,0:T(8,128)(2,1)S(1)}, u32[]{:S(2)}) copy-start(bf16[24,16,1024]{2,1,0:T(8,128)(2,1)S(1)} %collective-permute-done.7.refs_4_) | copy-start | bytes 2359300
  49.6 17.6 %collective-permute-start.13 = (bf16[16,16,1024]{2,1,0:T(8,128)(2,1)S(1)}, bf16[16,16,1024]{2,1,0:T(8,128)(2,1)S(1)}, u32[]{:S(2)}, u32[]{:S(2)}) collective-permute-start(bf16[16,16,1024]{2,1,0:T(8,128)(2,1)S(1)} %get-tuple-element.153), channel_id=1, source_target_pairs={{0,4},{1,5},{2,6},{3,7},{4,8},{5,9},{6,10},{7,11},{8,12},{9,13},{1... | collective-permute-start | bytes 1572872 | tf_op jit(solution)/shard_map/ppermute | solution.py:684
  52.1 17.0 %collective-permute-start.14 = (bf16[16,16,1024]{2,1,0:T(8,128)(2,1)S(1)}, bf16[16,16,1024]{2,1,0:T(8,128)(2,1)}, u32[]{:S(2)}, u32[]{:S(2)}) collective-permute-start(bf16[16,16,1024]{2,1,0:T(8,128)(2,1)S(1)} %get-tuple-element.154), channel_id=1, source_target_pairs={{4,0},{5,1},{6,2},{7,3},{8,4},{9,5},{10,6},{11,7},{12,8},{13,9},{1... | collective-permute-start | bytes 1572872 | tf_op jit(solution)/shard_map/ppermute | solution.py:684
  58.3 10.8 %copy-start.20 = (bf16[16,16,1024]{2,1,0:T(8,128)(2,1)}, bf16[16,16,1024]{2,1,0:T(8,128)(2,1)S(1)}, u32[]{:S(2)}) copy-start(bf16[16,16,1024]{2,1,0:T(8,128)(2,1)S(1)} %collective-permute-done.10.refs_7_) | copy-start | bytes 1572868
  58.3 10.8 %copy-start.24 = (bf16[16,16,1024]{2,1,0:T(8,128)(2,1)}, bf16[16,16,1024]{2,1,0:T(8,128)(2,1)S(1)}, u32[]{:S(2)}) copy-start(bf16[16,16,1024]{2,1,0:T(8,128)(2,1)S(1)} %collective-permute-done.11.refs_8_) | copy-start | bytes 1572868
  59.4 33.5 %collective-permute-start.17 = (bf16[24,16,1024]{2,1,0:T(8,128)(2,1)S(1)}, bf16[24,16,1024]{2,1,0:T(8,128)(2,1)}, u32[]{:S(2)}, u32[]{:S(2)}) collective-permute-start(bf16[24,16,1024]{2,1,0:T(8,128)(2,1)S(1)} %get-tuple-element.158), channel_id=1, source_target_pairs={{0,2},{1,3},{2,0},{3,1},{4,6},{5,7},{6,4},{7,5},{8,10},{9,11},{10,... | collective-permute-start | bytes 2359304 | tf_op jit(solution)/shard_map/ppermute | solution.py:684
  59.5 17.5 %collective-permute-start.15 = (bf16[16,16,1024]{2,1,0:T(8,128)(2,1)S(1)}, bf16[16,16,1024]{2,1,0:T(8,128)(2,1)S(1)}, u32[]{:S(2)}, u32[]{:S(2)}) collective-permute-start(bf16[16,16,1024]{2,1,0:T(8,128)(2,1)S(1)} %get-tuple-element.156), channel_id=1, source_target_pairs={{0,4},{1,5},{2,6},{3,7},{4,8},{5,9},{6,10},{7,11},{8,12},{9,13},{1... | collective-permute-start | bytes 1572872 | tf_op jit(solution)/shard_map/ppermute | solution.py:684
  67.2 3.8 %copy-start.28 = (bf16[16,16,1024]{2,1,0:T(8,128)(2,1)}, bf16[16,16,1024]{2,1,0:T(8,128)(2,1)S(1)}, u32[]{:S(2)}) copy-start(bf16[16,16,1024]{2,1,0:T(8,128)(2,1)S(1)} %collective-permute-done.13.refs_10_) | copy-start | bytes 1572868
  67.2 14.4 %collective-permute-start.16 = (bf16[16,16,1024]{2,1,0:T(8,128)(2,1)S(1)}, bf16[16,16,1024]{2,1,0:T(8,128)(2,1)S(1)}, u32[]{:S(2)}, u32[]{:S(2)}) collective-permute-start(bf16[16,16,1024]{2,1,0:T(8,128)(2,1)S(1)} %get-tuple-element.157), channel_id=1, source_target_pairs={{4,0},{5,1},{6,2},{7,3},{8,4},{9,5},{10,6},{11,7},{12,8},{13,9},{1... | collective-permute-start | bytes 1572872 | tf_op jit(solution)/shard_map/ppermute | solution.py:684
  69.1 23.7 %copy-start.11 = (bf16[24,16,1024]{2,1,0:T(8,128)(2,1)}, bf16[24,16,1024]{2,1,0:T(8,128)(2,1)S(1)}, u32[]{:S(2)}) copy-start(bf16[24,16,1024]{2,1,0:T(8,128)(2,1)S(1)} %collective-permute-done.12.refs_9_) | copy-start | bytes 2359300
  71.0 14.5 %collective-permute-start.18 = (bf16[16,16,1024]{2,1,0:T(8,128)(2,1)S(1)}, bf16[16,16,1024]{2,1,0:T(8,128)(2,1)S(1)}, u32[]{:S(2)}, u32[]{:S(2)}) collective-permute-start(bf16[16,16,1024]{2,1,0:T(8,128)(2,1)S(1)} %get-tuple-element.160.refs_14_), channel_id=1, source_target_pairs={{0,4},{1,5},{2,6},{3,7},{4,8},{5,9},{6,10},{7,11},{8,12},{9,13},{1... | collective-permute-start | bytes 1572872 | tf_op jit(solution)/shard_map/ppermute | solution.py:684
  74.9 18.0 %copy-start.21 = (bf16[16,16,1024]{2,1,0:T(8,128)(2,1)S(1)}, bf16[16,16,1024]{2,1,0:T(8,128)(2,1)}, u32[]{:S(2)}) copy-start(bf16[16,16,1024]{2,1,0:T(8,128)(2,1)} %copy-done.20) | copy-start | bytes 1572868
  74.9 18.0 %copy-start.25 = (bf16[16,16,1024]{2,1,0:T(8,128)(2,1)S(1)}, bf16[16,16,1024]{2,1,0:T(8,128)(2,1)}, u32[]{:S(2)}) copy-start(bf16[16,16,1024]{2,1,0:T(8,128)(2,1)} %copy-done.24) | copy-start | bytes 1572868
  74.9 18.0 %copy-start.29 = (bf16[16,16,1024]{2,1,0:T(8,128)(2,1)S(1)}, bf16[16,16,1024]{2,1,0:T(8,128)(2,1)}, u32[]{:S(2)}) copy-start(bf16[16,16,1024]{2,1,0:T(8,128)(2,1)} %copy-done.28) | copy-start | bytes 1572868
  74.9 17.9 %collective-permute-start.19 = (bf16[16,16,1024]{2,1,0:T(8,128)(2,1)S(1)}, bf16[16,16,1024]{2,1,0:T(8,128)(2,1)S(1)}, u32[]{:S(2)}, u32[]{:S(2)}) collective-permute-start(bf16[16,16,1024]{2,1,0:T(8,128)(2,1)S(1)} %get-tuple-element.161), channel_id=1, source_target_pairs={{4,0},{5,1},{6,2},{7,3},{8,4},{9,5},{10,6},{11,7},{12,8},{13,9},{1... | collective-permute-start | bytes 1572872 | tf_op jit(solution)/shard_map/ppermute | solution.py:684
  77.0 15.9 %copy-start.32 = (bf16[16,16,1024]{2,1,0:T(8,128)(2,1)}, bf16[16,16,1024]{2,1,0:T(8,128)(2,1)S(1)}, u32[]{:S(2)}) copy-start(bf16[16,16,1024]{2,1,0:T(8,128)(2,1)S(1)} %collective-permute-done.15.refs_12_) | copy-start | bytes 1572868
  81.6 11.3 %copy-start.35 = (bf16[16,16,1024]{2,1,0:T(8,128)(2,1)}, bf16[16,16,1024]{2,1,0:T(8,128)(2,1)S(1)}, u32[]{:S(2)}) copy-start(bf16[16,16,1024]{2,1,0:T(8,128)(2,1)S(1)} %collective-permute-done.16.refs_13_) | copy-start | bytes 1572868
  85.6 9.2 %copy-start.40 = (bf16[16,16,1024]{2,1,0:T(8,128)(2,1)}, bf16[16,16,1024]{2,1,0:T(8,128)(2,1)S(1)}, u32[]{:S(2)}) copy-start(bf16[16,16,1024]{2,1,0:T(8,128)(2,1)S(1)} %collective-permute-done.18.refs_15_) | copy-start | bytes 1572868
  94.8 12.2 %collective-permute-start.26 = (bf16[16,16,1024]{2,1,0:T(8,128)(2,1)S(1)}, bf16[16,16,1024]{2,1,0:T(8,128)(2,1)}, u32[]{:S(2)}, u32[]{:S(2)}) collective-permute-start(bf16[16,16,1024]{2,1,0:T(8,128)(2,1)S(1)} %get-tuple-element.164.refs_19_), channel_id=1, source_target_pairs={{0,4},{1,5},{2,6},{3,7},{4,8},{5,9},{6,10},{7,11},{8,12},{9,13},{1... | collective-permute-start | bytes 1572872 | tf_op jit(solution)/shard_map/ppermute | solution.py:684
  98.6 26.0 %collective-permute-start.20 = (bf16[16,16,1024]{2,1,0:T(8,128)(2,1)S(1)}, bf16[16,16,1024]{2,1,0:T(8,128)(2,1)}, u32[]{:S(2)}, u32[]{:S(2)}) collective-permute-start(bf16[16,16,1024]{2,1,0:T(8,128)(2,1)S(1)} %get-tuple-element.162.refs_17_), channel_id=1, source_target_pairs={{0,4},{1,5},{2,6},{3,7},{4,8},{5,9},{6,10},{7,11},{8,12},{9,13},{1... | collective-permute-start | bytes 1572872 | tf_op jit(solution)/shard_map/ppermute | solution.py:684
  100.5 24.1 %collective-permute-start.21 = (bf16[16,16,1024]{2,1,0:T(8,128)(2,1)S(1)}, bf16[16,16,1024]{2,1,0:T(8,128)(2,1)}, u32[]{:S(2)}, u32[]{:S(2)}) collective-permute-start(bf16[16,16,1024]{2,1,0:T(8,128)(2,1)S(1)} %get-tuple-element.163), channel_id=1, source_target_pairs={{4,0},{5,1},{6,2},{7,3},{8,4},{9,5},{10,6},{11,7},{12,8},{13,9},{1... | collective-permute-start | bytes 1572872 | tf_op jit(solution)/shard_map/ppermute | solution.py:684
  107.0 48.7 %all-to-all-start.1 = ((bf16[16,112,128]{2,1,0:T(8,128)(2,1)}), bf16[16,112,128]{2,1,0:T(8,128)(2,1)S(1)}, u32[]{:S(2)}, u32[]{:S(2)}) async-start(bf16[16,112,128]{2,1,0:T(8,128)(2,1)} %attend_3.1.refs_12_), calls=%async_computation.1 | async-start | bytes 917504 | tf_op jit(solution)/shard_map/all_to_all | solution.py:726
  120.8 17.5 %collective-permute-start.25 = (bf16[16,16,1024]{2,1,0:T(8,128)(2,1)S(1)}, bf16[16,16,1024]{2,1,0:T(8,128)(2,1)S(1)}, u32[]{:S(2)}, u32[]{:S(2)}) collective-permute-start(bf16[16,16,1024]{2,1,0:T(8,128)(2,1)S(1)} %get-tuple-element.168), channel_id=1, source_target_pairs={{0,2},{1,3},{2,0},{3,1},{4,6},{5,7},{6,4},{7,5},{8,10},{9,11},{10,... | collective-permute-start | bytes 1572872 | tf_op jit(solution)/shard_map/ppermute | solution.py:684
  121.0 22.9 %collective-permute-start.27 = (bf16[16,16,1024]{2,1,0:T(8,128)(2,1)}, bf16[16,16,1024]{2,1,0:T(8,128)(2,1)S(1)}, u32[]{:S(2)}, u32[]{:S(2)}) collective-permute-start(bf16[16,16,1024]{2,1,0:T(8,128)(2,1)} %get-tuple-element.169), channel_id=1, source_target_pairs={{4,0},{5,1},{6,2},{7,3},{8,4},{9,5},{10,6},{11,7},{12,8},{13,9},{1... | collective-permute-start | bytes 1572872 | tf_op jit(solution)/shard_map/ppermute | solution.py:684
  123.0 26.5 %copy-start.3 = (bf16[24,16,1024]{2,1,0:T(8,128)(2,1)S(1)}, bf16[24,16,1024]{2,1,0:T(8,128)(2,1)}, u32[]{:S(2)}) copy-start(bf16[24,16,1024]{2,1,0:T(8,128)(2,1)} %copy-done.2) | copy-start | bytes 2359300
  123.0 26.5 %copy-start.6 = (bf16[16,16,1024]{2,1,0:T(8,128)(2,1)S(1)}, bf16[16,16,1024]{2,1,0:T(8,128)(2,1)}, u32[]{:S(2)}) copy-start(bf16[16,16,1024]{2,1,0:T(8,128)(2,1)} %copy-done.5) | copy-start | bytes 1572868
  123.0 26.5 %copy-start.9 = (bf16[16,16,1024]{2,1,0:T(8,128)(2,1)S(1)}, bf16[16,16,1024]{2,1,0:T(8,128)(2,1)}, u32[]{:S(2)}) copy-start(bf16[16,16,1024]{2,1,0:T(8,128)(2,1)} %copy-done.8) | copy-start | bytes 1572868
  123.0 26.5 %copy-start.12 = (bf16[24,16,1024]{2,1,0:T(8,128)(2,1)S(1)}, bf16[24,16,1024]{2,1,0:T(8,128)(2,1)}, u32[]{:S(2)}) copy-start(bf16[24,16,1024]{2,1,0:T(8,128)(2,1)} %copy-done.11) | copy-start | bytes 2359300
  123.1 26.5 %copy-start.15 = (bf16[16,16,1024]{2,1,0:T(8,128)(2,1)S(1)}, bf16[16,16,1024]{2,1,0:T(8,128)(2,1)}, u32[]{:S(2)}) copy-start(bf16[16,16,1024]{2,1,0:T(8,128)(2,1)} %copy-done.14) | copy-start | bytes 1572868
  123.1 26.5 %copy-start.18 = (bf16[16,16,1024]{2,1,0:T(8,128)(2,1)S(1)}, bf16[16,16,1024]{2,1,0:T(8,128)(2,1)}, u32[]{:S(2)}) copy-start(bf16[16,16,1024]{2,1,0:T(8,128)(2,1)} %copy-done.17) | copy-start | bytes 1572868
  123.1 26.5 %copy-start.22 = (bf16[16,16,1024]{2,1,0:T(8,128)(2,1)S(1)}, bf16[16,16,1024]{2,1,0:T(8,128)(2,1)}, u32[]{:S(2)}) copy-start(bf16[16,16,1024]{2,1,0:T(8,128)(2,1)} %copy-done.20) | copy-start | bytes 1572868
  123.1 26.5 %copy-start.26 = (bf16[16,16,1024]{2,1,0:T(8,128)(2,1)S(1)}, bf16[16,16,1024]{2,1,0:T(8,128)(2,1)}, u32[]{:S(2)}) copy-start(bf16[16,16,1024]{2,1,0:T(8,128)(2,1)} %copy-done.24) | copy-start | bytes 1572868
  123.1 26.5 %copy-start.30 = (bf16[16,16,1024]{2,1,0:T(8,128)(2,1)S(1)}, bf16[16,16,1024]{2,1,0:T(8,128)(2,1)}, u32[]{:S(2)}) copy-start(bf16[16,16,1024]{2,1,0:T(8,128)(2,1)} %copy-done.28) | copy-start | bytes 1572868
  123.1 26.5 %copy-start.33 = (bf16[16,16,1024]{2,1,0:T(8,128)(2,1)S(1)}, bf16[16,16,1024]{2,1,0:T(8,128)(2,1)}, u32[]{:S(2)}) copy-start(bf16[16,16,1024]{2,1,0:T(8,128)(2,1)} %copy-done.32) | copy-start | bytes 1572868
  123.1 26.5 %copy-start.36 = (bf16[16,16,1024]{2,1,0:T(8,128)(2,1)S(1)}, bf16[16,16,1024]{2,1,0:T(8,128)(2,1)}, u32[]{:S(2)}) copy-start(bf16[16,16,1024]{2,1,0:T(8,128)(2,1)} %copy-done.35) | copy-start | bytes 1572868
  123.1 26.5 %copy-start.41 = (bf16[16,16,1024]{2,1,0:T(8,128)(2,1)S(1)}, bf16[16,16,1024]{2,1,0:T(8,128)(2,1)}, u32[]{:S(2)}) copy-start(bf16[16,16,1024]{2,1,0:T(8,128)(2,1)} %copy-done.40) | copy-start | bytes 1572868
  123.1 26.5 %copy-start.44 = (bf16[16,16,1024]{2,1,0:T(8,128)(2,1)S(1)}, bf16[16,16,1024]{2,1,0:T(8,128)(2,1)}, u32[]{:S(2)}) copy-start(bf16[16,16,1024]{2,1,0:T(8,128)(2,1)} %copy-done.43) | copy-start | bytes 1572868
  123.1 26.4 %collective-permute-start.28 = (bf16[16,16,1024]{2,1,0:T(8,128)(2,1)S(1)}, bf16[16,16,1024]{2,1,0:T(8,128)(2,1)S(1)}, u32[]{:S(2)}, u32[]{:S(2)}) collective-permute-start(bf16[16,16,1024]{2,1,0:T(8,128)(2,1)S(1)} %get-tuple-element.170), channel_id=1, source_target_pairs={{0,2},{1,3},{2,0},{3,1},{4,6},{5,7},{6,4},{7,5},{8,10},{9,11},{10,... | collective-permute-start | bytes 1572872 | tf_op jit(solution)/shard_map/ppermute | solution.py:684
  127.1 30.4 %collective-permute-start.22 = (bf16[16,16,1024]{2,1,0:T(8,128)(2,1)S(1)}, bf16[16,16,1024]{2,1,0:T(8,128)(2,1)}, u32[]{:S(2)}, u32[]{:S(2)}) collective-permute-start(bf16[16,16,1024]{2,1,0:T(8,128)(2,1)S(1)} %get-tuple-element.165.refs_23_.after), channel_id=1, source_target_pairs={{0,4},{1,5},{2,6},{3,7},{4,8},{5,9},{6,10},{7,11},{8,12},{9,13},{1... | collective-permute-start | bytes 1572872 | tf_op jit(solution)/shard_map/ppermute | solution.py:684
  130.4 27.1 %collective-permute-start.23 = (bf16[16,16,1024]{2,1,0:T(8,128)(2,1)}, bf16[16,16,1024]{2,1,0:T(8,128)(2,1)}, u32[]{:S(2)}, u32[]{:S(2)}) collective-permute-start(bf16[16,16,1024]{2,1,0:T(8,128)(2,1)} %get-tuple-element.166), channel_id=1, source_target_pairs={{4,0},{5,1},{6,2},{7,3},{8,4},{9,5},{10,6},{11,7},{12,8},{13,9},{1... | collective-permute-start | bytes 1572872 | tf_op jit(solution)/shard_map/ppermute | solution.py:684
  138.3 14.1 %copy-start.46 = (bf16[16,16,1024]{2,1,0:T(8,128)(2,1)}, bf16[16,16,1024]{2,1,0:T(8,128)(2,1)S(1)}, u32[]{:S(2)}) copy-start(bf16[16,16,1024]{2,1,0:T(8,128)(2,1)S(1)} %collective-permute-done.25.refs_19_) | copy-start | bytes 1572868
  138.3 19.2 %collective-permute-start.24 = (bf16[8,16,1024]{2,1,0:T(8,128)(2,1)S(1)}, bf16[8,16,1024]{2,1,0:T(8,128)(2,1)}, u32[]{:S(2)}, u32[]{:S(2)}) collective-permute-start(bf16[8,16,1024]{2,1,0:T(8,128)(2,1)S(1)} %get-tuple-element.167), channel_id=1, source_target_pairs={{0,2},{1,3},{2,0},{3,1},{4,6},{5,7},{6,4},{7,5},{8,10},{9,11},{10,... | collective-permute-start | bytes 786440 | tf_op jit(solution)/shard_map/ppermute | solution.py:684
  144.0 8.5 %copy-start.48 = (bf16[16,16,1024]{2,1,0:T(8,128)(2,1)}, bf16[16,16,1024]{2,1,0:T(8,128)(2,1)S(1)}, u32[]{:S(2)}) copy-start(bf16[16,16,1024]{2,1,0:T(8,128)(2,1)S(1)} %collective-permute-done.27.refs_21_) | copy-start | bytes 1572868
  149.6 2.8 %copy-start.50 = (bf16[16,16,1024]{2,1,0:T(8,128)(2,1)}, bf16[16,16,1024]{2,1,0:T(8,128)(2,1)S(1)}, u32[]{:S(2)}) copy-start(bf16[16,16,1024]{2,1,0:T(8,128)(2,1)S(1)} %collective-permute-done.28.refs_22_) | copy-start | bytes 1572868
  158.8 6.7 %collective-permute-start.29 = (bf16[64,16,1024]{2,1,0:T(8,128)(2,1)S(1)}, bf16[64,16,1024]{2,1,0:T(8,128)(2,1)S(1)}, u32[]{:S(2)}, u32[]{:S(2)}) collective-permute-start(bf16[64,16,1024]{2,1,0:T(8,128)(2,1)S(1)} %gather_give.5.refs_5_), channel_id=1, source_target_pairs={{0,1},{1,0},{2,3},{3,2},{4,5},{5,4},{6,7},{7,6},{8,9},{9,8},{10,11... | collective-permute-start | bytes 6291464 | tf_op jit(solution)/shard_map/ppermute | solution.py:701
  (6 other events, 13.0 us)
